TPU v7x, 512 devices: a whole 4x4x16 slice. The times are simulated.
512 devices in a mesh: section: 4 (over y), tok: 32 (over z, core), voc: 4 (over x).
Axes of the slice: x: 4, y: 4, z: 16, core: 2. Of those that a mesh axis runs over, the one named last changes fastest.
Arguments:
- hidden: bfloat16 [512, 4096], P(('tok', 'voc'), 'section'), may hold values from -1.4 to 1.4
- norm_gain: float32 [4096], P('section'), may hold values from 0.5 to 1.5
- value_weight: float32 [4096], P('section'), may hold values from -0.09375 to 0.09375
- head_weight: bfloat16 [98304, 4096], P(('tok', 'voc'), 'section'), may hold values from -0.3 to 0.3
- targets: int32 [512], P('section'), may hold values from 0 to 98303
- response_mask: int32 [512], P(('tok', 'voc')), may hold values 0 or 1
- loss_weight: float32 [512], P(('tok', 'voc')), may hold values from -1.5 to 1.5
- value_target: float32 [512], P(('tok', 'voc')), may hold values from -5 to 5
Outputs:
- logprobs: float32 [512], P('section')
- values: float32 [512], P(('tok', 'voc'))
- hidden_grad: bfloat16 [512, 4096], P(('tok', 'voc'), 'section')
All inputs are finite; a program needn't handle non-finite values. No bound on the sum of `response_mask` on one device may be relied on, other than what follows from the above.
Results may differ from a plain program's by a relative error of at most 0.0039.
Values may be sent and summed in bfloat16 or wider, within the bound.
No kernel may reach another device: no remote copies, remote signals or barrier semaphores. Data moves between devices by JAX's collectives and lax.ppermute only.
A program may use at most 64 MiB of HBM per device.

v0:
```python
import jax
import jax.numpy as jnp
from jax import lax
from jax.sharding import PartitionSpec as P

epsilon = 1e-06


def shards(
    hidden, norm_gain, value_weight, head_weight, targets, response_mask, loss_weight, value_target
):
    hidden_rows = hidden.astype(jnp.float32)
    full_width = hidden.shape[1] * lax.axis_size("section")
    squares = lax.psum(jnp.sum(hidden_rows * hidden_rows, axis=1), "section")
    inverse = lax.rsqrt(squares / full_width + epsilon)
    normed = hidden_rows * inverse[:, None] * norm_gain[None, :]
    values = lax.psum(jnp.sum(normed * value_weight[None, :], axis=1), "section")
    rounded = normed.astype(jnp.bfloat16)
    gathered = lax.all_gather(rounded, ("tok", "voc"), axis=0, tiled=True)
    logits = lax.psum_scatter(
        lax.dot_general(
            gathered, head_weight, (((1,), (1,)), ((), ())), preferred_element_type=jnp.float32
        ),
        "section",
        scatter_dimension=0,
        tiled=True,
    )
    shard_rows = head_weight.shape[0]
    offset = lax.axis_index(("tok", "voc")) * shard_rows
    columns = offset + lax.broadcasted_iota(jnp.int32, (1, shard_rows), 1)
    matches = columns == targets[:, None]
    local_max = jnp.max(logits, axis=1)
    picked = jnp.sum(jnp.where(matches, logits, jnp.zeros_like(logits)), axis=1)
    highest = lax.pmax(local_max, ("tok", "voc"))
    summed_exp, target_logit = lax.psum(
        (jnp.sum(jnp.exp(logits - highest[:, None]), axis=1), picked), ("tok", "voc")
    )
    log_norm = highest + jnp.log(summed_exp)
    logprobs = target_logit - log_norm
    errors = (jnp.exp(logits - log_norm[:, None]) - matches.astype(jnp.float32)).astype(
        jnp.bfloat16
    )
    partial_value = jnp.dot(
        lax.all_gather(errors, "section", axis=0, tiled=True),
        head_weight,
        preferred_element_type=jnp.float32,
    )
    summed = lax.psum_scatter(partial_value, ("tok", "voc"), scatter_dimension=0, tiled=True)
    value_error = values - value_target
    live = response_mask.astype(jnp.float32)
    cotangent = live[:, None] * (
        loss_weight[:, None] * summed + value_error[:, None] * value_weight[None, :]
    )
    scaled = norm_gain[None, :] * cotangent
    inner_sum = lax.psum(jnp.sum(hidden_rows * scaled, axis=1), "section")
    hidden_grad = (
        inverse[:, None] * scaled
        - hidden_rows * (inverse * inverse * inverse * inner_sum / full_width)[:, None]
    )
    return (logprobs, values, hidden_grad.astype(jnp.bfloat16))


def solution(mesh):
    in_specs = (
        P(("tok", "voc"), "section"),
        P("section"),
        P("section"),
        P(("tok", "voc"), "section"),
        P("section"),
        P(("tok", "voc")),
        P(("tok", "voc")),
        P(("tok", "voc")),
    )
    out_specs = (P("section"), P(("tok", "voc")), P(("tok", "voc"), "section"))
    return jax.shard_map(shards, mesh=mesh, in_specs=in_specs, out_specs=out_specs, check_vma=False)
```

profile of v0, /device:TPU:2, one launch (start us, length us, event | category | flops | bytes accessed | tf_op | source)
XLA Modules:
  0.0 1067.1 jit_solution(11946782495229322619)
XLA Ops:
  7.2 0.0 copy-start
  7.2 0.0 all-gather.3.cloned.1.call-start
  7.2 0.9 fusion.3
  8.2 10.7 %psum.35 = f32[4]{0:T(128)S(1)} all-reduce(f32[4]{0:T(128)S(1)} %fusion.3), channel_id=1, replica_groups=mesh['section'=4,'tok'=32,'voc'=4] {'section'}, use_global_device_ids=true, to_apply=%region_1.0 | all-reduce | flops 4 | bytes 32 | tf_op jit(solution)/shard_map/psum | solution.py:14
  18.9 1.5 fusion.7
  20.4 0.0 all-gather.3.cloned.1.call-update
  20.4 0.0 reduce-scatter.2.cloned.1.call-start
  20.5 132.9 %all-gather.3.cloned.1.call-done = bf16[128,4,1024]{2,1,0:T(4,128)(2,1)} async-done(((bf16[1,4,1024]{2,1,0:T(4,128)(2,1)}), bf16[128,4,1024]{2,1,0:T(4,128)(2,1)}) %all-gather.3.cloned.1.call-update) | async-done | bytes 1048592 | tf_op jit(solution)/shard_map/all_gather | solution.py:19
  153.4 1.3 reshape.22
  154.7 0.0 copy-done
  154.7 2.2 fusion.19
  156.9 0.0 copy-start.4
  156.9 0.0 reduce-scatter.2.cloned.1.call-update
  156.9 0.0 all-reduce.4.cloned.1.call-start
  157.0 29.2 %reduce-scatter.2.cloned.1.call-done = f32[128,768]{1,0:T(8,128)} async-done(((f32[512,768]{1,0:T(8,128)}), f32[128,768]{1,0:T(8,128)}) %reduce-scatter.2.cloned.1.call-update) | async-done | bytes 393232 | tf_op jit(solution)/shard_map/reduce_scatter | solution.py:20
  186.2 1.1 reduce_max.9
  187.3 247.8 %pmax.7 = f32[128]{0:T(128)S(1)} all-reduce(f32[128]{0:T(128)S(1)} %reduce_max.9), channel_id=1, replica_groups=mesh['section'=4,'tok'=32,'voc'=4] {'tok','voc'}, use_global_device_ids=true, to_apply=%region_6.7 | all-reduce | flops 128 | bytes 1024 | tf_op jit(solution)/shard_map/pmax | solution.py:34
  435.1 0.0 copy-done.4
  435.1 1.2 exponential_reduce_fusion
  436.3 251.2 %all-reduce.1 = (f32[128]{0:T(128)S(1)}, f32[128]{0:T(128)S(1)}) all-reduce(f32[128]{0:T(128)S(1)} %get-tuple-element.4, f32[128]{0:T(128)S(1)} %get-tuple-element.3), channel_id=1, replica_groups=mesh['section'=4,'tok'=32,'voc'=4] {'tok','voc'}, use_global_device_ids=true, to_apply=%region_4.0 | all-reduce | flops 256 | bytes 2048 | tf_op jit(solution)/shard_map/psum | solution.py:35
  687.6 0.5 fusion.18
  688.1 1.1 fusion.2
  689.2 13.4 %all_gather.7 = bf16[512,768]{1,0:T(8,128)(2,1)S(1)} all-gather(bf16[128,768]{1,0:T(8,128)(2,1)S(1)} %fusion.2), channel_id=1, replica_groups=mesh['section'=4,'tok'=32,'voc'=4] {'section'}, dimensions={0}, use_global_device_ids=true | all-gather | bytes 983040 | tf_op jit(solution)/shard_map/all_gather | solution.py:44
  702.6 2.3 fusion.20
  704.9 0.0 copy-start.6
  704.9 0.0 copy-start.7
  704.9 0.0 copy-start.1
  704.9 0.0 copy-start.2
  704.9 0.0 copy-start.3
  704.9 0.0 copy-start.5
  704.9 0.0 all-reduce.4.cloned.1.call-update
  704.9 9.9 psum.38
  714.9 0.0 copy-start.8
  714.9 0.0 copy-done.6
  714.9 0.0 copy-done.7
  714.9 1.3 dynamic-slice
  716.8 331.6 %all-reduce.4.cloned.1.call-done = f32[512,1024]{1,0:T(8,128)} async-done(((f32[512,1024]{1,0:T(8,128)}), f32[512,1024]{1,0:T(8,128)}) %all-reduce.4.cloned.1.call-update) | async-done | bytes 2097168
  1048.4 0.0 copy-done.1
  1048.4 0.0 copy-done.2
  1048.4 0.0 copy-done.3
  1048.4 0.0 copy-done.5
  1048.4 1.0 fusion.8
  1049.4 10.5 psum.39
  1059.9 0.7 fusion.10
  1060.5 0.0 copy-done.8
  (5 shorter events, 0.0 us)
Async XLA Ops:
  7.2 147.6 %copy-start = (bf16[768,1024]{1,0:T(8,128)(2,1)S(1)}, bf16[768,1024]{1,0:T(8,128)(2,1)}, u32[]{:S(2)}) copy-start(bf16[768,1024]{1,0:T(8,128)(2,1)} %param.11) | copy-start | bytes 4718596
  7.2 146.2 %all-gather.3.cloned.1.call-start = ((), (), s32[]{:S(2)}) async-start(), calls=%async_computation.2 | async-start | bytes 1056768 | tf_op jit(solution)/shard_map/all_gather | solution.py:19
  20.4 165.7 %reduce-scatter.2.cloned.1.call-start = ((), (), s32[]{:S(2)}) async-start(), calls=%async_computation.1 | async-start | bytes 1966080 | tf_op jit(solution)/shard_map/reduce_scatter | solution.py:20
  156.9 278.2 %copy-start.4 = (s32[128]{0:T(128)S(1)}, s32[128]{0:T(128)}, u32[]{:S(2)}) copy-start(s32[128]{0:T(128)} %param.12) | copy-start | bytes 1540
  156.9 891.5 %all-reduce.4.cloned.1.call-start = ((), (), s32[]{:S(2)}) async-start(), calls=%async_computation.3 | async-start | bytes 4194304
  704.9 10.0 copy-start.6
  704.9 10.0 copy-start.7
  704.9 343.5 %copy-start.1 = (bf16[4,1024]{1,0:T(4,128)(2,1)S(1)}, bf16[4,1024]{1,0:T(4,128)(2,1)}, u32[]{:S(2)}) copy-start(bf16[4,1024]{1,0:T(4,128)(2,1)} %param.8) | copy-start | bytes 24580
  704.9 343.5 %copy-start.2 = (f32[1024]{0:T(1024)S(1)}, f32[1024]{0:T(1024)}, u32[]{:S(2)}) copy-start(f32[1024]{0:T(1024)} %param.10) | copy-start | bytes 12292
  704.9 343.5 %copy-start.3 = (f32[1024]{0:T(1024)S(1)}, f32[1024]{0:T(1024)}, u32[]{:S(2)}) copy-start(f32[1024]{0:T(1024)} %param.9) | copy-start | bytes 12292
  704.9 343.5 %copy-start.5 = (f32[4]{0:T(128)S(1)}, f32[4]{0:T(128)}, u32[]{:S(2)}) copy-start(f32[4]{0:T(128)} %param.14) | copy-start | bytes 52
  714.9 345.7 %copy-start.8 = (f32[4]{0:T(128)}, f32[4]{0:T(128)S(1)}, u32[]{:S(2)}) copy-start(f32[4]{0:T(128)S(1)} %psum.38) | copy-start | bytes 52
Sparse Core Ops, SparseCore 0:
  20.6 132.7 all-gather.2
  157.1 29.0 reduce-scatter.1
  705.1 343.2 all-reduce.3
where the time goes:
time: 1070 us
  blocking collectives  544 us (51%)
  waiting for transfers between devices  494 us (46%)
  between operations  14.5 us (1%)
    unnamed x4, waiting for transfers between devices  332 us
    psum x1, blocking collectives, shards(): lax.psum((jnp.sum(jnp.exp(logits - highest[:, None]), axis=1), picked), (...  251 us
    pmax x1, blocking collectives, shards(): highest = lax.pmax(local_max, ('tok', 'voc'))  248 us
    all_gather x1, waiting for transfers between devices, shards(): gathered = lax.all_gather(rounded, ('tok', 'voc'), axis=0, tiled=True)  133 us
    reduce_scatter x1, waiting for transfers between devices, shards(): lax.psum_scatter(lax.dot_general(gathered, head_weight, (((1,), (1,)), ((...  29.2 us
  transfers between devices with their start and end apart: 3, of which 3 were waited for; matrix products, arithmetic and copies ran while one was open for 0% of the time, Pallas kernels for 0%

commit v1 on v0

v1 whole, which is shorter than its diff:
```python
import jax
import jax.numpy as jnp
from jax import lax
from jax.sharding import PartitionSpec as P

epsilon = 1e-06
bf16 = jnp.bfloat16
f32 = jnp.float32


def spread(array, axis):
    size = lax.axis_size(axis)
    copies = jnp.broadcast_to(array[None], (size,) + array.shape)
    return lax.all_to_all(copies, axis, 0, 0)


def exchange(array, axis):
    return lax.all_to_all(array, axis, 0, 0)


def shards(
    hidden, norm_gain, value_weight, head_weight, targets, response_mask, loss_weight, value_target
):
    width = hidden.shape[1]
    vocab = head_weight.shape[0]
    full_width = width * lax.axis_size("section")
    hidden_rows = hidden.astype(f32)
    scaled_rows = hidden_rows * norm_gain[None, :]
    squares, raw_values = lax.psum(
        (jnp.sum(hidden_rows * hidden_rows, axis=1), jnp.sum(scaled_rows * value_weight[None, :], axis=1)),
        "section",
    )
    inverse = lax.rsqrt(squares / full_width + epsilon)
    values = inverse * raw_values
    rounded = (hidden_rows * inverse[:, None] * norm_gain[None, :]).astype(bf16)

    by_z = spread(rounded, "z")
    by_x = lax.all_gather(by_z, "x", axis=0)
    other = lax.ppermute(by_x, "core", [(0, 1), (1, 0)])
    first = lax.axis_index("core") == 0
    gathered = jnp.stack([jnp.where(first, by_x, other), jnp.where(first, other, by_x)])
    rows = gathered.reshape(2, 4, 4, 16, width).transpose(2, 0, 1, 3, 4).reshape(512, width)
    partial = lax.dot_general(
        rows, head_weight, (((1,), (1,)), ((), ())), preferred_element_type=f32
    ).astype(bf16)
    parts = exchange(partial.reshape(4, 128, vocab), "section")
    logits = jnp.sum(parts.astype(f32), axis=0)

    shard = (lax.axis_index("z") * 2 + lax.axis_index("core")) * 4 + lax.axis_index("x")
    wanted = targets.reshape(4, 2, 4, 4).transpose(1, 2, 0, 3).reshape(128)
    columns = shard * vocab + lax.broadcasted_iota(jnp.int32, (1, vocab), 1)
    matches = columns == wanted[:, None]
    local_max = jnp.max(logits, axis=1)
    local_sum = jnp.sum(jnp.exp(logits - local_max[:, None]), axis=1)
    picked = jnp.sum(jnp.where(matches, logits, jnp.zeros_like(logits)), axis=1)

    def combine(stats):
        top = jnp.max(stats[:, 0], axis=0)
        total = jnp.sum(jnp.exp(stats[:, 0] - top[None]) * stats[:, 1], axis=0)
        return jnp.stack([top, total, jnp.sum(stats[:, 2], axis=0)])

    stats = combine(spread(jnp.stack([local_max, local_sum, picked]), ("core", "x")))
    stats = combine(spread(stats, "z"))
    log_norm = stats[0] + jnp.log(stats[1])
    logprobs = (stats[2] - log_norm).reshape(2, 4, 4, 4).transpose(2, 0, 1, 3).reshape(128)
    errors = (jnp.exp(logits - log_norm[:, None]) - matches.astype(f32)).astype(bf16)
    every = lax.all_gather(errors, "section", axis=0, tiled=True)
    back = jnp.dot(every, head_weight, preferred_element_type=f32)
    back = back.astype(bf16).reshape(4, 2, 4, 16, width).transpose(1, 2, 0, 3, 4)
    back = jnp.sum(exchange(back.reshape(2, 256, width), "core").astype(f32), axis=0).astype(bf16)
    back = jnp.sum(exchange(back.reshape(4, 64, width), "x").astype(f32), axis=0).astype(bf16)
    back = jnp.sum(exchange(back.reshape(16, 4, width), "z").astype(f32), axis=0)

    live = response_mask.astype(f32)
    cotangent = live[:, None] * (
        loss_weight[:, None] * back + (values - value_target)[:, None] * value_weight[None, :]
    )
    scaled = norm_gain[None, :] * cotangent
    inner_sum = lax.psum(jnp.sum(hidden_rows * scaled, axis=1), "section")
    hidden_grad = (
        inverse[:, None] * scaled
        - hidden_rows * (inverse * inverse * inverse * inner_sum / full_width)[:, None]
    )
    return (logprobs, values, hidden_grad.astype(bf16))


def solution(mesh):
    fine = jax.sharding.Mesh(
        mesh.devices.reshape(4, 16, 2, 4), ("section", "z", "core", "x")
    )
    group = ("z", "core", "x")
    in_specs = (
        P(group, "section"),
        P("section"),
        P("section"),
        P(group, "section"),
        P("section"),
        P(group),
        P(group),
        P(group),
    )
    out_specs = (P("section"), P(group), P(group, "section"))
    return jax.shard_map(shards, mesh=fine, in_specs=in_specs, out_specs=out_specs, check_vma=False)
```

time: 1070 us -> 167 us (0.16)
  the two profiles are of different devices: /device:TPU:2 before, /device:TPU:8 now
where the time goes in v1:
time: 167 us
  blocking collectives  116 us (69%)
  waiting for transfers between devices  26.3 us (16%)
  starting transfers between devices  11.5 us (7%)
  other arithmetic  5.84 us (3%)
  local copies, waits for them, and re-layouts  3.09 us (2%)
  matrix products  2.89 us (2%)
    all_to_all x3, blocking collectives, spread(): return lax.all_to_all(copies, axis, 0, 0)  48.2 us
    all_to_all x2, waiting for transfers between devices, exchange(): return lax.all_to_all(array, axis, 0, 0)  24.5 us
    all_to_all x2, blocking collectives, exchange(): return lax.all_to_all(array, axis, 0, 0)  17.2 us
    all_gather x1, blocking collectives, shards(): by_x = lax.all_gather(by_z, 'x', axis=0)  13.6 us
    psum x1, blocking collectives, shards(): lax.psum((jnp.sum(hidden_rows * hidden_rows, axis=1), jnp.sum(scaled_rows...  13.6 us
    all_gather x1, blocking collectives, shards(): every = lax.all_gather(errors, 'section', axis=0, tiled=True)  13.4 us
    psum x1, blocking collectives, shards(): inner_sum = lax.psum(jnp.sum(hidden_rows * scaled, axis=1), 'section')  10.1 us
    all_to_all x2, starting transfers between devices, exchange(): return lax.all_to_all(array, axis, 0, 0)  9.6 us
  transfers between devices with their start and end apart: 3, of which 3 were waited for; matrix products, arithmetic and copies ran while one was open for 1% of the time, Pallas kernels for 0%

profile of v1, /device:TPU:8, one launch (start us, length us, event | category | flops | bytes accessed | tf_op | source)
XLA Modules:
  0.0 166.6 jit_solution(1417377465689819123)
XLA Ops:
  0.6 0.0 copy-start
  0.6 1.0 fusion.7
  1.6 13.6 %all-reduce = (f32[4]{0:T(128)S(1)}, f32[4]{0:T(128)S(1)}) all-reduce(f32[4]{0:T(128)S(1)} %get-tuple-element.6, f32[4]{0:T(128)S(1)} %get-tuple-element.5), channel_id=1, replica_groups=mesh['section'=4,'z'=16,'core'=2,'x'=4] {'section'}, use_global_device_ids=true, to_apply=%region_1.0 | all-reduce | flops 8 | bytes 64 | tf_op jit(solution)/shard_map/psum | solution.py:29
  15.2 1.2 fusion.14
  16.4 0.8 fusion.5
  17.2 23.4 %all_to_all.35 = bf16[16,4,1024]{2,1,0:T(4,128)(2,1)S(1)} all-to-all(bf16[16,4,1024]{2,1,0:T(4,128)(2,1)S(1)} %broadcast_in_dim.8), channel_id=1, replica_groups=mesh['section'=4,'z'=16,'core'=2,'x'=4] {'z'}, dimensions={0} | all-to-all | bytes 262144 | tf_op jit(solution)/shard_map/all_to_all | solution.py:14
  40.6 13.6 %all-gather = bf16[64,4,1024]{2,0,1:T(8,128)(2,1)S(1)} all-gather(bf16[16,4,1024]{2,0,1:T(8,128)(2,1)S(1)} %copy.63), channel_id=2, replica_groups=mesh['section'=4,'z'=16,'core'=2,'x'=4] {'x'}, dimensions={0}, use_global_device_ids=true | all-gather | bytes 655360 | tf_op jit(solution)/shard_map/all_gather | solution.py:38
  54.3 1.9 %collective-permute-start = (bf16[4,16,4,1024]{3,1,0,2:T(8,128)(2,1)S(1)}, bf16[4,16,4,1024]{3,1,0,2:T(8,128)(2,1)S(1)}, u32[]{:S(2)}, u32[]{:S(2)}) collective-permute-start(bf16[4,16,4,1024]{3,1,0,2:T(8,128)(2,1)S(1)} %bitcast.35), channel_id=1, source_target_pairs={{0,4},{4,0},{1,5},{5,1},{2,6},{6,2},{3,7},{7,3},{8,12},{12,8},{9,1... | collective-permute-start | bytes 1572872 | tf_op jit(solution)/shard_map/ppermute | solution.py:39
  56.2 1.9 %collective-permute-done = bf16[4,16,4,1024]{3,1,0,2:T(8,128)(2,1)S(1)} collective-permute-done((bf16[4,16,4,1024]{3,1,0,2:T(8,128)(2,1)S(1)}, bf16[4,16,4,1024]{3,1,0,2:T(8,128)(2,1)S(1)}, u32[]{:S(2)}, u32[]{:S(2)}) %collective-permute-start) | collective-permute-done | bytes 524320 | tf_op jit(solution)/shard_map/ppermute | solution.py:39
  58.1 0.1 broadcast_select_fusion.1
  58.1 0.4 copy.65
  58.5 0.4 copy.64
  59.0 0.7 maximum_bitcast_fusion
  59.7 0.3 copy.66
  60.1 1.9 %convolution_convert_fusion.1 = bf16[512,768]{1,0:T(8,128)(2,1)} fusion(bf16[512,1024]{1,0:T(8,128)(2,1)S(1)} %bitcast.40, bf16[768,1024]{1,0:T(8,128)(2,1)S(1)} %copy-done), kind=kOutput, calls=%fused_computation.2 | convolution fusion | flops 805699584 | bytes 3407872 | tf_op jit(solution)/shard_map/dot_general | solution.py:43
  62.0 6.1 %all-to-all-start.1 = ((bf16[4,128,768]{2,1,0:T(8,128)(2,1)}), bf16[4,128,768]{2,1,0:T(8,128)(2,1)S(1)}, u32[]{:S(2)}, u32[]{:S(2)}) async-start(bf16[4,128,768]{2,1,0:T(8,128)(2,1)} %bitcast.5), calls=%async_computation.1 | async-start | bytes 1572864 | tf_op jit(solution)/shard_map/all_to_all | solution.py:18
  68.1 0.1 reshape.69
  68.2 0.1 eq.20
  68.3 11.1 %all-to-all-done.1 = bf16[4,128,768]{2,1,0:T(8,128)(2,1)S(1)} async-done(((bf16[4,128,768]{2,1,0:T(8,128)(2,1)}), bf16[4,128,768]{2,1,0:T(8,128)(2,1)S(1)}, u32[]{:S(2)}, u32[]{:S(2)}) %all-to-all-start.1) | async-done | bytes 786464 | tf_op jit(solution)/shard_map/all_to_all | solution.py:18
  79.5 0.1 convert_reduce_fusion
  79.6 0.1 reduce_max.27
  79.7 0.3 exponential_reduce_fusion
  80.0 8.8 %all_to_all.36 = f32[8,3,128]{2,1,0:T(4,128)S(1)} all-to-all(f32[8,3,128]{2,1,0:T(4,128)S(1)} %broadcast_in_dim.10), channel_id=1, replica_groups=mesh['section'=4,'z'=16,'core'=2,'x'=4] {'core','x'}, dimensions={0} | all-to-all | bytes 24576 | tf_op jit(solution)/shard_map/all_to_all | solution.py:14
  88.9 16.0 %all_to_all.37 = f32[16,3,128]{2,1,0:T(4,128)S(1)} all-to-all(f32[16,3,128]{2,1,0:T(4,128)S(1)} %broadcast_in_dim.11), channel_id=1, replica_groups=mesh['section'=4,'z'=16,'core'=2,'x'=4] {'z'}, dimensions={0} | all-to-all | bytes 49152 | tf_op jit(solution)/shard_map/all_to_all | solution.py:14
  104.9 0.2 fusion.2
  105.1 13.4 %all_gather.11 = bf16[512,768]{1,0:T(8,128)(2,1)S(1)} all-gather(bf16[128,768]{1,0:T(8,128)(2,1)S(1)} %fusion.2), channel_id=1, replica_groups=mesh['section'=4,'z'=16,'core'=2,'x'=4] {'section'}, dimensions={0}, use_global_device_ids=true | all-gather | bytes 983040 | tf_op jit(solution)/shard_map/all_gather | solution.py:67
  118.5 1.0 convolution_convert_fusion
  119.5 0.1 copy.73
  119.6 4.6 %all_to_all.38 = bf16[2,256,1024]{2,1,0:T(8,128)(2,1)S(1)} all-to-all(bf16[2,256,1024]{2,1,0:T(8,128)(2,1)S(1)} %bitcast.34), channel_id=1, replica_groups=mesh['section'=4,'z'=16,'core'=2,'x'=4] {'core'}, dimensions={0} | all-to-all | bytes 2097152 | tf_op jit(solution)/shard_map/all_to_all | solution.py:18
  124.2 0.2 reduce_sum.132
  124.4 0.0 copy-start.1
  124.4 0.0 copy-start.2
  124.4 0.0 copy-start.3
  124.4 0.0 copy-start.4
  124.5 12.6 %all_to_all.39 = bf16[4,64,1024]{2,1,0:T(8,128)(2,1)S(1)} all-to-all(bf16[4,64,1024]{2,1,0:T(8,128)(2,1)S(1)} %bitcast.37), channel_id=1, replica_groups=mesh['section'=4,'z'=16,'core'=2,'x'=4] {'x'}, dimensions={0} | all-to-all | bytes 1048576 | tf_op jit(solution)/shard_map/all_to_all | solution.py:18
  137.0 0.1 reduce_sum.133
  137.1 0.7 reshape.74
  137.8 3.5 %all-to-all-start.6 = ((bf16[16,4,1024]{2,1,0:T(4,128)(2,1)}), bf16[16,4,1024]{2,1,0:T(4,128)(2,1)S(1)}, u32[]{:S(2)}, u32[]{:S(2)}) async-start(bf16[16,4,1024]{2,1,0:T(4,128)(2,1)} %reshape.74), calls=%async_computation.6 | async-start | bytes 262144 | tf_op jit(solution)/shard_map/all_to_all | solution.py:18
  141.3 0.0 copy-done.6
  141.4 0.1 sub.55
  141.5 0.6 reshape.70
  142.1 13.3 %all-to-all-done.6 = bf16[16,4,1024]{2,1,0:T(4,128)(2,1)S(1)} async-done(((bf16[16,4,1024]{2,1,0:T(4,128)(2,1)}), bf16[16,4,1024]{2,1,0:T(4,128)(2,1)S(1)}, u32[]{:S(2)}, u32[]{:S(2)}) %all-to-all-start.6) | async-done | bytes 131104 | tf_op jit(solution)/shard_map/all_to_all | solution.py:18
  155.4 0.1 convert_reduce_fusion.1
  155.5 0.0 copy-done.1
  155.5 0.0 copy-done.2
  155.6 0.2 fusion.8
  155.8 10.1 %psum.23 = f32[4]{0:T(128)S(1)} all-reduce(f32[4]{0:T(128)S(1)} %get-tuple-element.9), channel_id=1, replica_groups=mesh['section'=4,'z'=16,'core'=2,'x'=4] {'section'}, use_global_device_ids=true, to_apply=%region_18.19 | all-reduce | flops 4 | bytes 32 | tf_op jit(solution)/shard_map/psum | solution.py:79
  165.9 0.7 fusion.10
  (26 shorter events, 0.3 us)
Async XLA Ops:
  0.6 59.4 %copy-start = (bf16[768,1024]{1,0:T(8,128)(2,1)S(1)}, bf16[768,1024]{1,0:T(8,128)(2,1)}, u32[]{:S(2)}) copy-start(bf16[768,1024]{1,0:T(8,128)(2,1)} %param.11) | copy-start | bytes 4718596
  54.3 3.8 %collective-permute-start = (bf16[4,16,4,1024]{3,1,0,2:T(8,128)(2,1)S(1)}, bf16[4,16,4,1024]{3,1,0,2:T(8,128)(2,1)S(1)}, u32[]{:S(2)}, u32[]{:S(2)}) collective-permute-start(bf16[4,16,4,1024]{3,1,0,2:T(8,128)(2,1)S(1)} %bitcast.35), channel_id=1, source_target_pairs={{0,4},{4,0},{1,5},{5,1},{2,6},{6,2},{3,7},{7,3},{8,12},{12,8},{9,1... | collective-permute-start | bytes 1572872 | tf_op jit(solution)/shard_map/ppermute | solution.py:39
  62.0 6.1 %copy-start.5 = (s32[128]{0:T(128)S(1)}, s32[128]{0:T(128)}, u32[]{:S(2)}) copy-start(s32[128]{0:T(128)} %param.12) | copy-start | bytes 1540
  62.0 17.5 %all-to-all-start.1 = ((bf16[4,128,768]{2,1,0:T(8,128)(2,1)}), bf16[4,128,768]{2,1,0:T(8,128)(2,1)S(1)}, u32[]{:S(2)}, u32[]{:S(2)}) async-start(bf16[4,128,768]{2,1,0:T(8,128)(2,1)} %bitcast.5), calls=%async_computation.1 | async-start | bytes 1572864 | tf_op jit(solution)/shard_map/all_to_all | solution.py:18
  124.2 17.2 %copy-start.6 = (s32[4]{0:T(128)S(1)}, s32[4]{0:T(128)}, u32[]{:S(2)}) copy-start(s32[4]{0:T(128)} %param.13) | copy-start | bytes 52
  124.4 31.1 %copy-start.1 = (bf16[4,1024]{1,0:T(4,128)(2,1)S(1)}, bf16[4,1024]{1,0:T(4,128)(2,1)}, u32[]{:S(2)}) copy-start(bf16[4,1024]{1,0:T(4,128)(2,1)} %param.8) | copy-start | bytes 24580
  124.4 31.1 %copy-start.2 = (f32[1024]{0:T(1024)S(1)}, f32[1024]{0:T(1024)}, u32[]{:S(2)}) copy-start(f32[1024]{0:T(1024)} %param.9) | copy-start | bytes 12292
  124.4 31.1 %copy-start.3 = (f32[1024]{0:T(1024)S(1)}, f32[1024]{0:T(1024)}, u32[]{:S(2)}) copy-start(f32[1024]{0:T(1024)} %param.10) | copy-start | bytes 12292
  124.4 31.1 %copy-start.4 = (f32[4]{0:T(128)S(1)}, f32[4]{0:T(128)}, u32[]{:S(2)}) copy-start(f32[4]{0:T(128)} %param.14) | copy-start | bytes 52
  137.8 17.6 %all-to-all-start.6 = ((bf16[16,4,1024]{2,1,0:T(4,128)(2,1)}), bf16[16,4,1024]{2,1,0:T(4,128)(2,1)S(1)}, u32[]{:S(2)}, u32[]{:S(2)}) async-start(bf16[16,4,1024]{2,1,0:T(4,128)(2,1)} %reshape.74), calls=%async_computation.6 | async-start | bytes 262144 | tf_op jit(solution)/shard_map/all_to_all | solution.py:18

commit v2 on v1

v2 whole, which is shorter than its diff:
```python
import jax
import jax.numpy as jnp
from jax import lax
from jax.experimental import pallas as pl
from jax.experimental.pallas import tpu as pltpu
from jax.sharding import PartitionSpec as P

epsilon = 1e-06
bf16 = jnp.bfloat16
f32 = jnp.float32
WIDTH = 1024
VOCAB = 768
FULL = 4096
STATS = 2 * WIDTH
ROWS = STATS + 128
NT = (((1,), (1,)), ((), ()))
WAVE = 64 * 1024 * 1024 // 2


def two(value):
    high = value.astype(bf16).astype(f32)
    return [high, (value - high).astype(bf16).astype(f32)]


def three(value):
    high, low = value.astype(bf16).astype(f32), None
    return [high] + two(value - high)


def lanes(rows, columns):
    lane = lax.broadcasted_iota(jnp.int32, (rows, 128), 1)
    block = jnp.zeros((rows, 128), f32)
    for index, column in enumerate(columns):
        block = jnp.where(lane == index, column, block)
    return block


def take(block, first, last):
    lane = lax.broadcasted_iota(jnp.int32, block.shape, block.ndim - 1)
    kept = jnp.where((lane >= first) & (lane < last), block, 0.0)
    return jnp.sum(kept, axis=-1, keepdims=True)


def call(body, outs, *args, scratch=()):
    return pl.pallas_call(
        body,
        out_shape=[jax.ShapeDtypeStruct(shape, dtype) for shape, dtype in outs],
        scratch_shapes=list(scratch),
        compiler_params=pltpu.CompilerParams(vmem_limit_bytes=WAVE),
    )(*args)


def unit_of(exponent):
    return jnp.exp2(exponent)


def exponent_of(value):
    return jnp.floor(jnp.log2(jnp.maximum(value, 1e-30))) - 13.0


def digits(value):
    exponent = exponent_of(jnp.abs(value))
    scaled = value / unit_of(exponent)
    high = jnp.round(scaled)
    return [exponent, high, jnp.round((scaled - high) * 16384.0)]


def undigits(block, first):
    high, low = take(block, first + 1, first + 2), take(block, first + 2, first + 3)
    return (high + low / 16384.0) * unit_of(take(block, first, first + 1))


def project(own_ref, other_ref, gain_ref, value_ref, head_ref, out_ref):
    for half, ref in enumerate((own_ref, other_ref)):
        rows = ref[...].astype(f32)
        gained = rows * gain_ref[...]
        squares = jnp.sum(rows * rows, axis=1, keepdims=True)
        raw_values = jnp.sum(gained * value_ref[...], axis=1, keepdims=True)
        high = gained.astype(bf16)
        low = (gained - high.astype(f32)).astype(bf16)
        logits = lax.dot_general(high, head_ref[...], NT, preferred_element_type=f32)
        logits += lax.dot_general(low, head_ref[...], NT, preferred_element_type=f32)
        exponent = exponent_of(jnp.max(jnp.abs(logits), axis=1, keepdims=True))
        whole = jnp.round(logits * (1.0 / unit_of(exponent))).astype(jnp.int32).astype(jnp.int16)
        block = lanes(256, [exponent] + digits(squares) + digits(raw_values))
        block = block.astype(jnp.int32).astype(jnp.int16)
        for x in range(4):
            for s in range(4):
                source = slice(x * 64 + s * 16, x * 64 + s * 16 + 16)
                target = slice(half * 64 + x * 16, half * 64 + x * 16 + 16)
                out_ref[s, target, 0:VOCAB] = whole[source]
                out_ref[s, target, VOCAB:] = block[source]


def soften(core_ref, parts_ref, wanted_ref, out_ref, rows_ref):
    squares = raw_values = logits = 0.0
    for source in range(4):
        block = parts_ref[source, :, VOCAB:].astype(jnp.int32).astype(f32)
        whole = parts_ref[source, :, :VOCAB].astype(jnp.int32).astype(f32)
        logits = logits + whole * unit_of(take(block, 0, 1))
        squares = squares + undigits(block, 1)
        raw_values = raw_values + undigits(block, 4)
    inverse = lax.rsqrt(squares / FULL + epsilon)
    values = inverse * raw_values
    logits = logits * inverse
    column = lax.broadcasted_iota(jnp.int32, (128, VOCAB), 1)
    matches = column == wanted_ref[...]
    top = jnp.max(logits, axis=1, keepdims=True).astype(bf16).astype(f32)
    exps = jnp.exp(logits - top)
    total = jnp.sum(exps, axis=1, keepdims=True)
    first = jnp.sum(exps * logits, axis=1, keepdims=True)
    picked = jnp.sum(jnp.where(matches, logits, 0.0), axis=1, keepdims=True)
    out_ref[:, :VOCAB] = jnp.where(matches, -1.0, exps).astype(bf16)
    stats = [top] + two(total) + two(first) + two(picked) + three(inverse) + three(values)
    out_ref[:, VOCAB:] = lanes(128, stats).astype(bf16)
    pieces = lanes(128, [top] + two(total) + two(picked)).astype(bf16)
    place = lax.broadcasted_iota(jnp.int32, (128, 128), 0)
    natural = lax.broadcasted_iota(jnp.int32, (128, 128), 1)
    wanted_place = (
        ((natural // 16) % 2 ^ core_ref[0]) * 64
        + ((natural // 4) % 4) * 16
        + (natural // 32) * 4
        + natural % 4
    )
    moved = jnp.where(place == wanted_place, 1.0, 0.0).astype(bf16)
    rows_ref[...] = lax.dot_general(
        pieces, moved, (((0,), (0,)), ((), ())), preferred_element_type=f32
    )[0:16].astype(bf16)


def row_parts(top, total, picked):
    pieces = [top] + two(total) + two(picked)
    row = lax.broadcasted_iota(jnp.int32, (16, 128), 0)
    block = jnp.zeros((16, 128), f32)
    for index, piece in enumerate(pieces):
        block = jnp.where(row == index, piece, block)
    return block.astype(bf16)


def pull(exps_ref, head_ref, rows_ref, own_ref, other_ref):
    for half, ref in enumerate((own_ref, other_ref)):
        pieces = [
            exps_ref[s, half * 64 + x * 16 : half * 64 + x * 16 + 16]
            for x in range(4)
            for s in range(4)
        ]
        chosen = jnp.concatenate(pieces, axis=0)
        exps = chosen[:, :VOCAB].astype(f32)
        head = head_ref[...]
        ref[:, 0:WIDTH] = jnp.dot(
            jnp.maximum(exps, 0.0).astype(bf16), head, preferred_element_type=f32
        ).astype(bf16)
        ref[:, WIDTH:STATS] = jnp.dot(
            jnp.where(exps < 0.0, 1.0, 0.0).astype(bf16), head, preferred_element_type=f32
        ).astype(bf16)
        ref[:, STATS:ROWS] = chosen[:, VOCAB:]
        ref[:, ROWS:] = jnp.zeros((256, 128), bf16)
    other_ref[0:16, ROWS:] = rows_ref[...]


def read_rows(block):
    block = block.astype(f32)
    return block[0:1], block[1:2] + block[2:3], block[3:4] + block[4:5]


def read_lanes(block):
    block = block.astype(f32)
    return take(block, 0, 1), take(block, 1, 3), take(block, 3, 5), take(block, 5, 7)


def merge(pairs):
    top = pairs[0][0]
    for pair in pairs[1:]:
        top = jnp.maximum(top, pair[0])
    weights = [jnp.exp(pair[0] - top) for pair in pairs]
    total = weights[0] * pairs[0][1]
    for weight, pair in zip(weights[1:], pairs[1:]):
        total = total + weight * pair[1]
    return top, weights, total


def join(sources):
    stats = [read_lanes(source[1]) for source in sources]
    top, weights, total = merge(stats)
    first = sum(weight * stat[2] for weight, stat in zip(weights, stats))
    picked = sum(stat[3] for stat in stats)
    product = sum(
        weight * source[0].astype(f32) for weight, source in zip(weights, sources)
    )
    return product, top, total, first, picked


def join_rows(blocks):
    top, _, total = merge(blocks)
    return top, total, sum(block[2] for block in blocks)


def join_core(own_ref, got_ref, rows_ref, out_ref):
    product, top, total, first, picked = join(
        [(ref[:, 0:WIDTH], ref[:, STATS:ROWS]) for ref in (own_ref, got_ref)]
    )
    wanted = own_ref[:, WIDTH:STATS].astype(f32) + got_ref[:, WIDTH:STATS].astype(f32)
    block = row_parts(
        *join_rows([read_rows(rows_ref[...]), read_rows(got_ref[0:16, ROWS:])])
    )
    stats = lanes(256, [top] + two(total) + two(first) + two(picked)).astype(bf16)
    product, wanted = product.astype(bf16), wanted.astype(bf16)
    for x in range(4):
        out_ref[x, :, 0:WIDTH] = product[x * 64 : x * 64 + 64]
        out_ref[x, :, WIDTH:STATS] = wanted[x * 64 : x * 64 + 64]
        out_ref[x, :, STATS:ROWS] = stats[x * 64 : x * 64 + 64]
        out_ref[x, 0:16, ROWS:] = block
        out_ref[x, 16:64, ROWS:] = jnp.zeros((48, 128), bf16)


def join_x(got_ref, out_ref):
    product, top, total, first, picked = join(
        [(got_ref[k, :, 0:WIDTH], got_ref[k, :, STATS:ROWS]) for k in range(4)]
    )
    top_row, total_row, picked_row = join_rows(
        [read_rows(got_ref[k, 0:16, ROWS:]) for k in range(4)]
    )
    stats = lanes(64, [top] + two(total) + two(first) + two(picked))
    pieces = [top_row] + two(total_row) + two(picked_row)
    row = lax.broadcasted_iota(jnp.int32, (4, 128), 0)
    left = jnp.zeros((4, 128), f32)
    for index in range(4):
        left = jnp.where(row == index, pieces[index], left)
    right = jnp.where(row == 0, pieces[4], 0.0)
    wanted = sum(got_ref[k, :, WIDTH:STATS].astype(f32) for k in range(4))
    for z in range(16):
        some = slice(z * 4, z * 4 + 4)
        out_ref[z, :, 0:WIDTH] = product[some].astype(bf16)
        out_ref[z, :, WIDTH : 2 * WIDTH] = wanted[some].astype(bf16)
        out_ref[z, :, 2 * WIDTH : 2 * WIDTH + 128] = stats[some].astype(bf16)
        out_ref[z, :, 2 * WIDTH + 128 : 2 * WIDTH + 256] = left.astype(bf16)
        out_ref[z, :, 2 * WIDTH + 256 :] = right.astype(bf16)


def finish(
    got_ref, own_ref, hidden_ref, gain_ref, value_ref, token_ref, grad_ref, logprobs_ref
):
    product, top, total, first, picked = join(
        [
            (got_ref[k, :, 0:WIDTH], got_ref[k, :, 2 * WIDTH : 2 * WIDTH + 128])
            for k in range(16)
        ]
    )
    wanted = sum(got_ref[k, :, WIDTH : 2 * WIDTH].astype(f32) for k in range(16))
    log_norm = top + jnp.log(total)
    back = product / total + (jnp.exp(picked - log_norm) - 1.0) * wanted
    own = own_ref[...].astype(f32)
    inverse = take(own, 7, 10)
    values = take(own, 10, 13)
    token = token_ref[...]
    live, weight, value_target = token[:, 0:1], token[:, 1:2], token[:, 2:3]
    value_error = values - value_target
    cotangent = live * (weight * back + value_error * value_ref[...])
    inner = live * (weight * (first / total - picked) + value_error * values)
    rows = hidden_ref[...].astype(f32)
    grad_ref[...] = (
        inverse * gain_ref[...] * cotangent - rows * (inverse * inverse * inner / FULL)
    ).astype(bf16)
    blocks = []
    for k in range(16):
        left = got_ref[k, :, 2 * WIDTH + 128 : 2 * WIDTH + 256].astype(f32)
        right = got_ref[k, :, 2 * WIDTH + 256 :].astype(f32)
        blocks.append((left[0:1], left[1:2] + left[2:3], left[3:4] + right[0:1]))
    top_row, total_row, picked_row = join_rows(blocks)
    logprobs_ref[...] = picked_row - (top_row + jnp.log(total_row))


def spread(array, axis):
    size = lax.axis_size(axis)
    copies = jnp.broadcast_to(array[None], (size,) + array.shape)
    return lax.all_to_all(copies, axis, 0, 0)


def shards(
    hidden, norm_gain, value_weight, head_weight, targets, response_mask, loss_weight, value_target
):
    core = lax.axis_index("core")
    z, x = lax.axis_index("z"), lax.axis_index("x")
    shard = (z * 2 + core) * 4 + x
    gain, value_row = norm_gain[None, :], value_weight[None, :]
    swap = [(0, 1), (1, 0)]

    by_z = spread(hidden, "z")
    own = lax.all_gather(by_z, "x", axis=0).reshape(256, WIDTH)
    other = lax.ppermute(own, "core", swap)
    (sent,) = call(
        project, [((4, 128, VOCAB + 128), jnp.int16)], own, other, gain, value_row, head_weight
    )
    parts = lax.all_to_all(sent, "section", 0, 0)

    block = targets.reshape(4, 2, 4, 4).transpose(1, 2, 0, 3)
    block = jnp.where(core == 0, block, block[::-1]).reshape(128, 1) - shard * VOCAB
    exps, rows = pl.pallas_call(
        soften,
        out_shape=[
            jax.ShapeDtypeStruct((128, VOCAB + 128), bf16),
            jax.ShapeDtypeStruct((16, 128), bf16),
        ],
        in_specs=[
            pl.BlockSpec(memory_space=pltpu.SMEM),
            pl.BlockSpec(memory_space=pltpu.VMEM),
            pl.BlockSpec(memory_space=pltpu.VMEM),
        ],
        compiler_params=pltpu.CompilerParams(vmem_limit_bytes=WAVE),
    )(core.astype(jnp.int32).reshape(1), parts, block)
    every = lax.all_gather(exps, "section", axis=0)
    half = ((256, 2 * WIDTH + 256), bf16)
    mine, theirs = call(pull, [half, half], every, head_weight, rows)
    own_stats = lax.dynamic_slice(mine, (x * 64 + z * 4, STATS), (4, 128))
    got = lax.ppermute(theirs, "core", swap)
    (sent,) = call(join_core, [((4, 64, 2 * WIDTH + 256), bf16)], mine, got, rows)
    got = lax.all_to_all(sent, "x", 0, 0)
    (sent,) = call(join_x, [((16, 4, 2 * WIDTH + 384), bf16)], got)
    got = lax.all_to_all(sent, "z", 0, 0)
    token = jnp.stack([response_mask.astype(f32), loss_weight, value_target], axis=1)
    grad, logprobs = call(
        finish,
        [((4, WIDTH), bf16), ((1, 128), f32)],
        got,
        own_stats,
        hidden,
        gain,
        value_row,
        token,
    )
    values = jnp.sum(own_stats[:, 10:13].astype(f32), axis=1)
    return (logprobs.reshape(128), values, grad)


def solution(mesh):
    fine = jax.sharding.Mesh(
        mesh.devices.reshape(4, 16, 2, 4), ("section", "z", "core", "x")
    )
    group = ("z", "core", "x")
    in_specs = (
        P(group, "section"),
        P("section"),
        P("section"),
        P(group, "section"),
        P("section"),
        P(group),
        P(group),
        P(group),
    )
    out_specs = (P("section"), P(group), P(group, "section"))
    return jax.shard_map(shards, mesh=fine, in_specs=in_specs, out_specs=out_specs, check_vma=False)
```

time: 167 us -> 139 us (0.83)
  the two profiles are of different devices: /device:TPU:8 before, /device:TPU:32 now
where the time goes in v2:
time: 139 us
  blocking collectives  77.3 us (56%)
  waiting for transfers between devices  36.3 us (26%)
  starting transfers between devices  13.4 us (10%)
  Pallas kernels  8.88 us (6%)
  local copies, waits for them, and re-layouts  1.49 us (1%)
    all_to_all x1, blocking collectives, spread(): return lax.all_to_all(copies, axis, 0, 0)  29.2 us
    all_to_all x1, blocking collectives, shards(): got = lax.all_to_all(sent, 'x', 0, 0)  20.3 us
    all_to_all x1, waiting for transfers between devices, shards(): got = lax.all_to_all(sent, 'z', 0, 0)  17.8 us
    all_gather x1, blocking collectives, shards(): every = lax.all_gather(exps, 'section', axis=0)  14.7 us
    all_to_all x1, waiting for transfers between devices, shards(): parts = lax.all_to_all(sent, 'section', 0, 0)  13.7 us
    all_gather x1, blocking collectives, shards(): own = lax.all_gather(by_z, 'x', axis=0).reshape(256, WIDTH)  13.1 us
    pallas_call x5, Pallas kernels, call(): pl.pallas_call(body, out_shape=[jax.ShapeDtypeStruct(shape, dtype) for sh...  7.91 us
    all_to_all x1, starting transfers between devices, shards(): got = lax.all_to_all(sent, 'z', 0, 0)  4.94 us
  transfers between devices with their start and end apart: 4, of which 4 were waited for; matrix products, arithmetic and copies ran while one was open for 1% of the time, Pallas kernels for 0%

profile of v2, /device:TPU:32, one launch (start us, length us, event | category | flops | bytes accessed | tf_op | source)
XLA Modules:
  0.0 138.9 jit_solution(14565243761455275017)
XLA Ops:
  0.6 0.0 copy-start.2
  0.6 0.0 copy-start.3
  0.7 0.0 copy-start
  0.7 0.9 broadcast_in_dim.12
  1.5 29.2 %all_to_all.20 = bf16[16,4,1024]{2,1,0:T(4,128)(2,1)S(1)} all-to-all(bf16[16,4,1024]{2,1,0:T(4,128)(2,1)S(1)} %broadcast_in_dim.12), channel_id=1, replica_groups=mesh['section'=4,'z'=16,'core'=2,'x'=4] {'z'}, dimensions={0} | all-to-all | bytes 262144 | tf_op jit(solution)/shard_map/all_to_all | solution.py:276
  30.7 13.1 %all-gather = bf16[64,4,1024]{2,1,0:T(4,128)(2,1)S(1)} all-gather(bf16[16,4,1024]{2,1,0:T(4,128)(2,1)S(1)} %all_to_all.20), channel_id=2, replica_groups=mesh['section'=4,'z'=16,'core'=2,'x'=4] {'x'}, dimensions={0}, use_global_device_ids=true | all-gather | bytes 655360 | tf_op jit(solution)/shard_map/all_gather | solution.py:289
  43.9 0.1 reshape.35.own_ref
  44.0 1.9 %collective-permute-start = (bf16[256,1024]{1,0:T(8,128)(2,1)S(1)}, bf16[256,1024]{1,0:T(8,128)(2,1)S(1)}, u32[]{:S(2)}, u32[]{:S(2)}) collective-permute-start(bf16[256,1024]{1,0:T(8,128)(2,1)S(1)} %reshape.35.own_ref), channel_id=1, source_target_pairs={{0,4},{4,0},{1,5},{5,1},{2,6},{6,2},{3,7},{7,3},{8,12},{12,8},{9,1... | collective-permute-start | bytes 1572872 | tf_op jit(solution)/shard_map/ppermute | solution.py:290
  45.9 1.9 %collective-permute-done.other_ref = bf16[256,1024]{1,0:T(8,128)(2,1)S(1)} collective-permute-done((bf16[256,1024]{1,0:T(8,128)(2,1)S(1)}, bf16[256,1024]{1,0:T(8,128)(2,1)S(1)}, u32[]{:S(2)}, u32[]{:S(2)}) %collective-permute-start) | collective-permute-done | bytes 524320 | tf_op jit(solution)/shard_map/ppermute | solution.py:290
  47.8 0.0 copy-done.2
  47.8 0.0 copy-done.3
  47.8 0.0 copy-done
  47.8 3.2 %shard_map.103 = s16[4,128,896]{2,1,0:T(8,128)(2,1)} custom-call(bf16[256,1024]{1,0:T(8,128)(2,1)S(1)} %reshape.35.own_ref, bf16[256,1024]{1,0:T(8,128)(2,1)S(1)} %collective-permute-done.other_ref, f32[1,1024]{1,0:T(1,128)S(1)} %bitcast.11, f32[1,1024]{1,0:T(1,128)S(1)} %bitcast.13, bf16[768,1024]{1,0:T(8,128)(2,1)S(1)} %copy-done), custom_call_target="tpu_custom_call" | custom-call | tf_op jit(solution)/shard_map/pallas_call | solution.py:45
  51.0 0.0 copy-start.4
  51.0 4.6 %all-to-all-start.1 = ((s16[4,128,896]{2,1,0:T(8,128)(2,1)}), s16[4,128,896]{2,1,0:T(8,128)(2,1)S(1)}, u32[]{:S(2)}, u32[]{:S(2)}) async-start(s16[4,128,896]{2,1,0:T(8,128)(2,1)} %shard_map.103), calls=%async_computation.1 | async-start | bytes 1835008 | tf_op jit(solution)/shard_map/all_to_all | solution.py:294
  55.6 0.0 copy-done.4
  55.6 0.1 reshape.36
  55.8 0.1 sub.11.wanted_ref
  55.9 13.7 %all-to-all-done.1.parts_ref = s16[4,128,896]{2,1,0:T(8,128)(2,1)S(1)} async-done(((s16[4,128,896]{2,1,0:T(8,128)(2,1)}), s16[4,128,896]{2,1,0:T(8,128)(2,1)S(1)}, u32[]{:S(2)}, u32[]{:S(2)}) %all-to-all-start.1) | async-done | bytes 917536 | tf_op jit(solution)/shard_map/all_to_all | solution.py:294
  69.6 1.0 shard_map.104
  70.6 14.7 %all-gather.1 = bf16[512,896]{1,0:T(8,128)(2,1)S(1)} all-gather(bf16[128,896]{1,0:T(8,128)(2,1)S(1)} %get-tuple-element.9), channel_id=3, replica_groups=mesh['section'=4,'z'=16,'core'=2,'x'=4] {'section'}, dimensions={0}, use_global_device_ids=true | all-gather | bytes 1146880 | tf_op jit(solution)/shard_map/all_gather | solution.py:311
  85.3 1.8 %shard_map.105 = (bf16[256,2304]{1,0:T(8,128)(2,1)S(1)}, bf16[256,2304]{1,0:T(8,128)(2,1)S(1)}) custom-call(bf16[4,128,896]{2,1,0:T(8,128)(2,1)S(1)} %bitcast.10, bf16[768,1024]{1,0:T(8,128)(2,1)S(1)} %copy-done, bf16[16,128]{1,0:T(8,128)(2,1)S(1)} %get-tuple-element.10.rows_ref), custom_call_target="tpu_custom_call" | custom-call | tf_op jit(solution)/shard_map/pallas_call | solution.py:45
  87.1 1.9 %collective-permute-start.1 = (bf16[256,2304]{1,0:T(8,128)(2,1)S(1)}, bf16[256,2304]{1,0:T(8,128)(2,1)S(1)}, u32[]{:S(2)}, u32[]{:S(2)}) collective-permute-start(bf16[256,2304]{1,0:T(8,128)(2,1)S(1)} %get-tuple-element.12), channel_id=1, source_target_pairs={{0,4},{4,0},{1,5},{5,1},{2,6},{6,2},{3,7},{7,3},{8,12},{12,8},{9,1... | collective-permute-start | bytes 3538952 | tf_op jit(solution)/shard_map/ppermute | solution.py:315
  89.0 2.8 %collective-permute-done.1.got_ref = bf16[256,2304]{1,0:T(8,128)(2,1)S(1)} collective-permute-done((bf16[256,2304]{1,0:T(8,128)(2,1)S(1)}, bf16[256,2304]{1,0:T(8,128)(2,1)S(1)}, u32[]{:S(2)}, u32[]{:S(2)}) %collective-permute-start.1) | collective-permute-done | bytes 1179680 | tf_op jit(solution)/shard_map/ppermute | solution.py:315
  91.9 0.8 shard_map.106
  92.7 20.3 %all_to_all.21.got_ref = bf16[4,64,2304]{2,1,0:T(8,128)(2,1)S(1)} all-to-all(bf16[4,64,2304]{2,1,0:T(8,128)(2,1)S(1)} %shard_map.106), channel_id=1, replica_groups=mesh['section'=4,'z'=16,'core'=2,'x'=4] {'x'}, dimensions={0} | all-to-all | bytes 2359296 | tf_op jit(solution)/shard_map/all_to_all | solution.py:317
  113.0 0.0 copy-start.7
  113.0 0.0 copy-start.5
  113.0 0.0 copy-start.6
  113.0 0.0 copy-start.1
  113.0 1.1 shard_map.107
  114.1 4.9 %all-to-all-start.3 = ((bf16[16,4,2432]{2,1,0:T(4,128)(2,1)}), bf16[16,4,2432]{2,1,0:T(4,128)(2,1)S(1)}, u32[]{:S(2)}, u32[]{:S(2)}) async-start(bf16[16,4,2432]{2,1,0:T(4,128)(2,1)} %shard_map.107), calls=%async_computation.3 | async-start | bytes 622592 | tf_op jit(solution)/shard_map/all_to_all | solution.py:319
  119.0 0.0 copy-done.7
  119.0 0.1 copy.18
  119.1 0.0 copy-done.5
  119.1 0.1 copy.19
  119.2 0.0 copy-done.6
  119.2 0.1 copy.20
  119.3 0.1 pad_maximum_fusion.token_ref
  119.4 0.7 convert_reduce_fusion
  120.1 17.8 %all-to-all-done.3.got_ref = bf16[16,4,2432]{2,1,0:T(4,128)(2,1)S(1)} async-done(((bf16[16,4,2432]{2,1,0:T(4,128)(2,1)}), bf16[16,4,2432]{2,1,0:T(4,128)(2,1)S(1)}, u32[]{:S(2)}, u32[]{:S(2)}) %all-to-all-start.3) | async-done | bytes 311328 | tf_op jit(solution)/shard_map/all_to_all | solution.py:319
  137.9 0.0 copy-done.1
  137.9 0.9 shard_map.108
  (4 shorter events, 0.0 us)
Async XLA Ops:
  0.6 47.2 %copy-start.2 = (f32[1024]{0:T(1024)S(1)}, f32[1024]{0:T(1024)}, u32[]{:S(2)}) copy-start(f32[1024]{0:T(1024)} %param.9) | copy-start | bytes 12292
  0.6 47.2 %copy-start.3 = (f32[1024]{0:T(1024)S(1)}, f32[1024]{0:T(1024)}, u32[]{:S(2)}) copy-start(f32[1024]{0:T(1024)} %param.10) | copy-start | bytes 12292
  0.7 47.1 %copy-start = (bf16[768,1024]{1,0:T(8,128)(2,1)S(1)}, bf16[768,1024]{1,0:T(8,128)(2,1)}, u32[]{:S(2)}) copy-start(bf16[768,1024]{1,0:T(8,128)(2,1)} %head_ref.3) | copy-start | bytes 4718596
  44.0 3.8 %collective-permute-start = (bf16[256,1024]{1,0:T(8,128)(2,1)S(1)}, bf16[256,1024]{1,0:T(8,128)(2,1)S(1)}, u32[]{:S(2)}, u32[]{:S(2)}) collective-permute-start(bf16[256,1024]{1,0:T(8,128)(2,1)S(1)} %reshape.35.own_ref), channel_id=1, source_target_pairs={{0,4},{4,0},{1,5},{5,1},{2,6},{6,2},{3,7},{7,3},{8,12},{12,8},{9,1... | collective-permute-start | bytes 1572872 | tf_op jit(solution)/shard_map/ppermute | solution.py:290
  51.0 4.6 %copy-start.4 = (s32[128]{0:T(128)S(1)}, s32[128]{0:T(128)}, u32[]{:S(2)}) copy-start(s32[128]{0:T(128)} %param.12) | copy-start | bytes 1540
  51.0 18.6 %all-to-all-start.1 = ((s16[4,128,896]{2,1,0:T(8,128)(2,1)}), s16[4,128,896]{2,1,0:T(8,128)(2,1)S(1)}, u32[]{:S(2)}, u32[]{:S(2)}) async-start(s16[4,128,896]{2,1,0:T(8,128)(2,1)} %shard_map.103), calls=%async_computation.1 | async-start | bytes 1835008 | tf_op jit(solution)/shard_map/all_to_all | solution.py:294
  87.1 4.7 %collective-permute-start.1 = (bf16[256,2304]{1,0:T(8,128)(2,1)S(1)}, bf16[256,2304]{1,0:T(8,128)(2,1)S(1)}, u32[]{:S(2)}, u32[]{:S(2)}) collective-permute-start(bf16[256,2304]{1,0:T(8,128)(2,1)S(1)} %get-tuple-element.12), channel_id=1, source_target_pairs={{0,4},{4,0},{1,5},{5,1},{2,6},{6,2},{3,7},{7,3},{8,12},{12,8},{9,1... | collective-permute-start | bytes 3538952 | tf_op jit(solution)/shard_map/ppermute | solution.py:315
  113.0 6.1 %copy-start.7 = (s32[4]{0:T(128)S(1)}, s32[4]{0:T(128)}, u32[]{:S(2)}) copy-start(s32[4]{0:T(128)} %param.13) | copy-start | bytes 52
  113.0 6.2 %copy-start.5 = (f32[4]{0:T(128)S(1)}, f32[4]{0:T(128)}, u32[]{:S(2)}) copy-start(f32[4]{0:T(128)} %param.14) | copy-start | bytes 52
  113.0 6.3 %copy-start.6 = (f32[4]{0:T(128)S(1)}, f32[4]{0:T(128)}, u32[]{:S(2)}) copy-start(f32[4]{0:T(128)} %param.15) | copy-start | bytes 52
  113.0 25.0 %copy-start.1 = (bf16[4,1024]{1,0:T(4,128)(2,1)S(1)}, bf16[4,1024]{1,0:T(4,128)(2,1)}, u32[]{:S(2)}) copy-start(bf16[4,1024]{1,0:T(4,128)(2,1)} %hidden_ref.1) | copy-start | bytes 24580
  114.1 23.9 %all-to-all-start.3 = ((bf16[16,4,2432]{2,1,0:T(4,128)(2,1)}), bf16[16,4,2432]{2,1,0:T(4,128)(2,1)S(1)}, u32[]{:S(2)}, u32[]{:S(2)}) async-start(bf16[16,4,2432]{2,1,0:T(4,128)(2,1)} %shard_map.107), calls=%async_computation.3 | async-start | bytes 622592 | tf_op jit(solution)/shard_map/all_to_all | solution.py:319

commit v3 on v2

--- a/solution.py
+++ b/solution.py
@@ -14,7 +14,7 @@
 STATS = 2 * WIDTH
 ROWS = STATS + 128
 NT = (((1,), (1,)), ((), ()))
-WAVE = 64 * 1024 * 1024 // 2
+SCOPED = 32 * 1024 * 1024
 
 
 def two(value):
@@ -46,7 +46,7 @@
         body,
         out_shape=[jax.ShapeDtypeStruct(shape, dtype) for shape, dtype in outs],
         scratch_shapes=list(scratch),
-        compiler_params=pltpu.CompilerParams(vmem_limit_bytes=WAVE),
+        compiler_params=pltpu.CompilerParams(vmem_limit_bytes=SCOPED),
     )(*args)
 
 
@@ -70,26 +70,33 @@
     return (high + low / 16384.0) * unit_of(take(block, first, first + 1))
 
 
-def project(own_ref, other_ref, gain_ref, value_ref, head_ref, out_ref):
-    for half, ref in enumerate((own_ref, other_ref)):
-        rows = ref[...].astype(f32)
-        gained = rows * gain_ref[...]
-        squares = jnp.sum(rows * rows, axis=1, keepdims=True)
-        raw_values = jnp.sum(gained * value_ref[...], axis=1, keepdims=True)
-        high = gained.astype(bf16)
-        low = (gained - high.astype(f32)).astype(bf16)
-        logits = lax.dot_general(high, head_ref[...], NT, preferred_element_type=f32)
-        logits += lax.dot_general(low, head_ref[...], NT, preferred_element_type=f32)
-        exponent = exponent_of(jnp.max(jnp.abs(logits), axis=1, keepdims=True))
-        whole = jnp.round(logits * (1.0 / unit_of(exponent))).astype(jnp.int32).astype(jnp.int16)
-        block = lanes(256, [exponent] + digits(squares) + digits(raw_values))
-        block = block.astype(jnp.int32).astype(jnp.int16)
-        for x in range(4):
-            for s in range(4):
-                source = slice(x * 64 + s * 16, x * 64 + s * 16 + 16)
-                target = slice(half * 64 + x * 16, half * 64 + x * 16 + 16)
-                out_ref[s, target, 0:VOCAB] = whole[source]
-                out_ref[s, target, VOCAB:] = block[source]
+def encode(ref, gain_ref, value_ref, head_ref):
+    rows = ref[...].astype(f32)
+    gained = rows * gain_ref[...]
+    squares = jnp.sum(rows * rows, axis=1, keepdims=True)
+    raw_values = jnp.sum(gained * value_ref[...], axis=1, keepdims=True)
+    high = gained.astype(bf16)
+    low = (gained - high.astype(f32)).astype(bf16)
+    logits = lax.dot_general(high, head_ref[...], NT, preferred_element_type=f32)
+    logits += lax.dot_general(low, head_ref[...], NT, preferred_element_type=f32)
+    exponent = exponent_of(jnp.max(jnp.abs(logits), axis=1, keepdims=True))
+    whole = jnp.round(logits * (1.0 / unit_of(exponent))).astype(jnp.int32).astype(jnp.int16)
+    block = lanes(256, [exponent] + digits(squares) + digits(raw_values))
+    return whole, block.astype(jnp.int32).astype(jnp.int16)
+
+
+def project_own(own_ref, gain_ref, value_ref, head_ref, out_ref):
+    out_ref[:, :VOCAB], out_ref[:, VOCAB:] = encode(own_ref, gain_ref, value_ref, head_ref)
+
+
+def project(first_ref, other_ref, gain_ref, value_ref, head_ref, out_ref):
+    whole, block = encode(other_ref, gain_ref, value_ref, head_ref)
+    for x in range(4):
+        for s in range(4):
+            source = slice(x * 64 + s * 16, x * 64 + s * 16 + 16)
+            out_ref[s, x * 16 : x * 16 + 16] = first_ref[source]
+            out_ref[s, 64 + x * 16 : 64 + x * 16 + 16, :VOCAB] = whole[source]
+            out_ref[s, 64 + x * 16 : 64 + x * 16 + 16, VOCAB:] = block[source]
 
 
 def soften(core_ref, parts_ref, wanted_ref, out_ref, rows_ref):
@@ -137,25 +144,32 @@
     return block.astype(bf16)
 
 
-def pull(exps_ref, head_ref, rows_ref, own_ref, other_ref):
-    for half, ref in enumerate((own_ref, other_ref)):
-        pieces = [
-            exps_ref[s, half * 64 + x * 16 : half * 64 + x * 16 + 16]
-            for x in range(4)
-            for s in range(4)
-        ]
-        chosen = jnp.concatenate(pieces, axis=0)
-        exps = chosen[:, :VOCAB].astype(f32)
-        head = head_ref[...]
-        ref[:, 0:WIDTH] = jnp.dot(
-            jnp.maximum(exps, 0.0).astype(bf16), head, preferred_element_type=f32
-        ).astype(bf16)
-        ref[:, WIDTH:STATS] = jnp.dot(
-            jnp.where(exps < 0.0, 1.0, 0.0).astype(bf16), head, preferred_element_type=f32
-        ).astype(bf16)
-        ref[:, STATS:ROWS] = chosen[:, VOCAB:]
-        ref[:, ROWS:] = jnp.zeros((256, 128), bf16)
-    other_ref[0:16, ROWS:] = rows_ref[...]
+def pull(half, exps_ref, head_ref, out_ref):
+    pieces = [
+        exps_ref[s, half * 64 + x * 16 : half * 64 + x * 16 + 16]
+        for x in range(4)
+        for s in range(4)
+    ]
+    chosen = jnp.concatenate(pieces, axis=0)
+    exps = chosen[:, :VOCAB].astype(f32)
+    head = head_ref[...]
+    out_ref[:, 0:WIDTH] = jnp.dot(
+        jnp.maximum(exps, 0.0).astype(bf16), head, preferred_element_type=f32
+    ).astype(bf16)
+    out_ref[:, WIDTH:STATS] = jnp.dot(
+        jnp.where(exps < 0.0, 1.0, 0.0).astype(bf16), head, preferred_element_type=f32
+    ).astype(bf16)
+    out_ref[:, STATS:ROWS] = chosen[:, VOCAB:]
+
+
+def pull_own(exps_ref, head_ref, out_ref):
+    pull(0, exps_ref, head_ref, out_ref)
+
+
+def pull_other(exps_ref, head_ref, rows_ref, out_ref):
+    pull(1, exps_ref, head_ref, out_ref)
+    out_ref[0:16, ROWS:] = rows_ref[...]
+    out_ref[16:, ROWS:] = jnp.zeros((240, 128), bf16)
 
 
 def read_rows(block):
@@ -288,8 +302,16 @@
     by_z = spread(hidden, "z")
     own = lax.all_gather(by_z, "x", axis=0).reshape(256, WIDTH)
     other = lax.ppermute(own, "core", swap)
+    coded = (256, VOCAB + 128)
+    (first,) = call(project_own, [(coded, jnp.int16)], own, gain, value_row, head_weight)
     (sent,) = call(
-        project, [((4, 128, VOCAB + 128), jnp.int16)], own, other, gain, value_row, head_weight
+        project,
+        [((4, 128, VOCAB + 128), jnp.int16)],
+        first,
+        other,
+        gain,
+        value_row,
+        head_weight,
     )
     parts = lax.all_to_all(sent, "section", 0, 0)
 
@@ -306,13 +328,13 @@
             pl.BlockSpec(memory_space=pltpu.VMEM),
             pl.BlockSpec(memory_space=pltpu.VMEM),
         ],
-        compiler_params=pltpu.CompilerParams(vmem_limit_bytes=WAVE),
+        compiler_params=pltpu.CompilerParams(vmem_limit_bytes=SCOPED),
     )(core.astype(jnp.int32).reshape(1), parts, block)
     every = lax.all_gather(exps, "section", axis=0)
-    half = ((256, 2 * WIDTH + 256), bf16)
-    mine, theirs = call(pull, [half, half], every, head_weight, rows)
+    (theirs,) = call(pull_other, [((256, ROWS + 128), bf16)], every, head_weight, rows)
+    got = lax.ppermute(theirs, "core", swap)
+    (mine,) = call(pull_own, [((256, ROWS), bf16)], every, head_weight)
     own_stats = lax.dynamic_slice(mine, (x * 64 + z * 4, STATS), (4, 128))
-    got = lax.ppermute(theirs, "core", swap)
     (sent,) = call(join_core, [((4, 64, 2 * WIDTH + 256), bf16)], mine, got, rows)
     got = lax.all_to_all(sent, "x", 0, 0)
     (sent,) = call(join_x, [((16, 4, 2 * WIDTH + 384), bf16)], got)

time: 139 us -> 137 us (0.986)
  waiting for transfers between devices: 36.3 us -> 34 us
    pallas_call x5 -> x7, Pallas kernels: 7.91 us -> 8.24 us  [call(): pl.pallas_call(body, out_shape=[jax.ShapeDtypeStruct(shape, dtype) for sh...]
  transfers between devices with their start and end apart: 4 -> 4, of which waited for: 4 -> 4; matrix products, arithmetic and copies ran while one was open for 1% -> 1% of each run, Pallas kernels for 0% -> 2%
where the time goes in v3:
time: 137 us
  blocking collectives  77.3 us (56%)
  waiting for transfers between devices  34 us (25%)
  starting transfers between devices  13.4 us (10%)
  Pallas kernels  9.21 us (7%)
  local copies, waits for them, and re-layouts  1.49 us (1%)
    all_to_all x1, blocking collectives, spread(): return lax.all_to_all(copies, axis, 0, 0)  29.2 us
    all_to_all x1, blocking collectives, shards(): got = lax.all_to_all(sent, 'x', 0, 0)  20.3 us
    all_to_all x1, waiting for transfers between devices, shards(): got = lax.all_to_all(sent, 'z', 0, 0)  17.8 us
    all_gather x1, blocking collectives, shards(): every = lax.all_gather(exps, 'section', axis=0)  14.7 us
    all_to_all x1, waiting for transfers between devices, shards(): parts = lax.all_to_all(sent, 'section', 0, 0)  13.7 us
    all_gather x1, blocking collectives, shards(): own = lax.all_gather(by_z, 'x', axis=0).reshape(256, WIDTH)  13.1 us
    pallas_call x7, Pallas kernels, call(): pl.pallas_call(body, out_shape=[jax.ShapeDtypeStruct(shape, dtype) for sh...  8.24 us
    all_to_all x1, starting transfers between devices, shards(): got = lax.all_to_all(sent, 'z', 0, 0)  4.97 us
  transfers between devices with their start and end apart: 4, of which 4 were waited for; matrix products, arithmetic and copies ran while one was open for 1% of the time, Pallas kernels for 2%

profile of v3, /device:TPU:32, one launch (start us, length us, event | category | flops | bytes accessed | tf_op | source)
XLA Modules:
  0.0 137.0 jit_solution(15480796103340559662)
XLA Ops:
  0.6 0.0 copy-start.1
  0.6 0.0 copy-start.2
  0.7 0.0 copy-start
  0.7 0.9 broadcast_in_dim.12
  1.5 29.2 %all_to_all.20 = bf16[16,4,1024]{2,1,0:T(4,128)(2,1)S(1)} all-to-all(bf16[16,4,1024]{2,1,0:T(4,128)(2,1)S(1)} %broadcast_in_dim.12), channel_id=1, replica_groups=mesh['section'=4,'z'=16,'core'=2,'x'=4] {'z'}, dimensions={0} | all-to-all | bytes 262144 | tf_op jit(solution)/shard_map/all_to_all | solution.py:290
  30.7 13.1 %all-gather = bf16[64,4,1024]{2,1,0:T(4,128)(2,1)S(1)} all-gather(bf16[16,4,1024]{2,1,0:T(4,128)(2,1)S(1)} %all_to_all.20), channel_id=2, replica_groups=mesh['section'=4,'z'=16,'core'=2,'x'=4] {'x'}, dimensions={0}, use_global_device_ids=true | all-gather | bytes 655360 | tf_op jit(solution)/shard_map/all_gather | solution.py:303
  43.9 0.1 reshape.35.own_ref
  44.0 1.9 %collective-permute-start = (bf16[256,1024]{1,0:T(8,128)(2,1)S(1)}, bf16[256,1024]{1,0:T(8,128)(2,1)S(1)}, u32[]{:S(2)}, u32[]{:S(2)}) collective-permute-start(bf16[256,1024]{1,0:T(8,128)(2,1)S(1)} %reshape.35.own_ref), channel_id=1, source_target_pairs={{0,4},{4,0},{1,5},{5,1},{2,6},{6,2},{3,7},{7,3},{8,12},{12,8},{9,1... | collective-permute-start | bytes 1572872 | tf_op jit(solution)/shard_map/ppermute | solution.py:304
  45.9 0.0 copy-done.1
  45.9 0.0 copy-done.2
  45.9 0.0 copy-done
  45.9 1.2 shard_map.103.first_ref
  47.2 0.6 collective-permute-done.other_ref
  47.8 2.2 %shard_map.104 = s16[4,128,896]{2,1,0:T(8,128)(2,1)} custom-call(s16[256,896]{1,0:T(8,128)(2,1)S(1)} %shard_map.103.first_ref, bf16[256,1024]{1,0:T(8,128)(2,1)S(1)} %collective-permute-done.other_ref, f32[1,1024]{1,0:T(1,128)S(1)} %bitcast.13, f32[1,1024]{1,0:T(1,128)S(1)} %bitcast.16, bf16[768,1024]{1,0:T(8,128)(2,1)S(1)} %copy-done), custom_call_target="tpu_custom_call" | custom-call | tf_op jit(solution)/shard_map/pallas_call | solution.py:45
  50.0 0.0 copy-start.4
  50.0 4.6 %all-to-all-start.1 = ((s16[4,128,896]{2,1,0:T(8,128)(2,1)}), s16[4,128,896]{2,1,0:T(8,128)(2,1)S(1)}, u32[]{:S(2)}, u32[]{:S(2)}) async-start(s16[4,128,896]{2,1,0:T(8,128)(2,1)} %shard_map.104), calls=%async_computation.1 | async-start | bytes 1835008 | tf_op jit(solution)/shard_map/all_to_all | solution.py:316
  54.6 0.0 copy-done.4
  54.6 0.1 reshape.36
  54.7 0.1 sub.11.wanted_ref
  54.8 13.7 %all-to-all-done.1.parts_ref = s16[4,128,896]{2,1,0:T(8,128)(2,1)S(1)} async-done(((s16[4,128,896]{2,1,0:T(8,128)(2,1)}), s16[4,128,896]{2,1,0:T(8,128)(2,1)S(1)}, u32[]{:S(2)}, u32[]{:S(2)}) %all-to-all-start.1) | async-done | bytes 917536 | tf_op jit(solution)/shard_map/all_to_all | solution.py:316
  68.6 1.0 shard_map.105
  69.5 14.7 %all-gather.1 = bf16[512,896]{1,0:T(8,128)(2,1)S(1)} all-gather(bf16[128,896]{1,0:T(8,128)(2,1)S(1)} %get-tuple-element.7), channel_id=3, replica_groups=mesh['section'=4,'z'=16,'core'=2,'x'=4] {'section'}, dimensions={0}, use_global_device_ids=true | all-gather | bytes 1146880 | tf_op jit(solution)/shard_map/all_gather | solution.py:333
  84.2 1.0 shard_map.107
  85.2 1.9 %collective-permute-start.1 = (bf16[256,2304]{1,0:T(8,128)(2,1)S(1)}, bf16[256,2304]{1,0:T(8,128)(2,1)S(1)}, u32[]{:S(2)}, u32[]{:S(2)}) collective-permute-start(bf16[256,2304]{1,0:T(8,128)(2,1)S(1)} %shard_map.107), channel_id=1, source_target_pairs={{0,4},{4,0},{1,5},{5,1},{2,6},{6,2},{3,7},{7,3},{8,12},{12,8},{9,1... | collective-permute-start | bytes 3538952 | tf_op jit(solution)/shard_map/ppermute | solution.py:335
  87.1 1.0 shard_map.106.own_ref
  88.1 1.8 %collective-permute-done.1.got_ref = bf16[256,2304]{1,0:T(8,128)(2,1)S(1)} collective-permute-done((bf16[256,2304]{1,0:T(8,128)(2,1)S(1)}, bf16[256,2304]{1,0:T(8,128)(2,1)S(1)}, u32[]{:S(2)}, u32[]{:S(2)}) %collective-permute-start.1) | collective-permute-done | bytes 1179680 | tf_op jit(solution)/shard_map/ppermute | solution.py:335
  89.9 0.8 shard_map.108
  90.7 20.3 %all_to_all.21.got_ref = bf16[4,64,2304]{2,1,0:T(8,128)(2,1)S(1)} all-to-all(bf16[4,64,2304]{2,1,0:T(8,128)(2,1)S(1)} %shard_map.108), channel_id=1, replica_groups=mesh['section'=4,'z'=16,'core'=2,'x'=4] {'x'}, dimensions={0} | all-to-all | bytes 2359296 | tf_op jit(solution)/shard_map/all_to_all | solution.py:339
  111.1 0.0 copy-start.7
  111.1 0.0 copy-start.5
  111.1 0.0 copy-start.6
  111.1 0.0 copy-start.3
  111.1 1.1 shard_map.109
  112.2 5.0 %all-to-all-start.3 = ((bf16[16,4,2432]{2,1,0:T(4,128)(2,1)}), bf16[16,4,2432]{2,1,0:T(4,128)(2,1)S(1)}, u32[]{:S(2)}, u32[]{:S(2)}) async-start(bf16[16,4,2432]{2,1,0:T(4,128)(2,1)} %shard_map.109), calls=%async_computation.3 | async-start | bytes 622592 | tf_op jit(solution)/shard_map/all_to_all | solution.py:341
  117.2 0.0 copy-done.7
  117.2 0.1 copy.18
  117.3 0.0 copy-done.5
  117.3 0.1 copy.19
  117.4 0.0 copy-done.6
  117.4 0.1 copy.20
  117.5 0.1 pad_maximum_fusion.token_ref
  117.5 0.7 convert_reduce_fusion
  118.2 17.8 %all-to-all-done.3.got_ref = bf16[16,4,2432]{2,1,0:T(4,128)(2,1)S(1)} async-done(((bf16[16,4,2432]{2,1,0:T(4,128)(2,1)}), bf16[16,4,2432]{2,1,0:T(4,128)(2,1)S(1)}, u32[]{:S(2)}, u32[]{:S(2)}) %all-to-all-start.3) | async-done | bytes 311328 | tf_op jit(solution)/shard_map/all_to_all | solution.py:341
  136.1 0.0 copy-done.3
  136.1 0.9 shard_map.110
  (4 shorter events, 0.0 us)
Async XLA Ops:
  0.6 45.3 %copy-start.1 = (f32[1024]{0:T(1024)S(1)}, f32[1024]{0:T(1024)}, u32[]{:S(2)}) copy-start(f32[1024]{0:T(1024)} %param.9) | copy-start | bytes 12292
  0.6 45.3 %copy-start.2 = (f32[1024]{0:T(1024)S(1)}, f32[1024]{0:T(1024)}, u32[]{:S(2)}) copy-start(f32[1024]{0:T(1024)} %param.10) | copy-start | bytes 12292
  0.7 45.3 %copy-start = (bf16[768,1024]{1,0:T(8,128)(2,1)S(1)}, bf16[768,1024]{1,0:T(8,128)(2,1)}, u32[]{:S(2)}) copy-start(bf16[768,1024]{1,0:T(8,128)(2,1)} %head_ref.7) | copy-start | bytes 4718596
  44.0 3.8 %collective-permute-start = (bf16[256,1024]{1,0:T(8,128)(2,1)S(1)}, bf16[256,1024]{1,0:T(8,128)(2,1)S(1)}, u32[]{:S(2)}, u32[]{:S(2)}) collective-permute-start(bf16[256,1024]{1,0:T(8,128)(2,1)S(1)} %reshape.35.own_ref), channel_id=1, source_target_pairs={{0,4},{4,0},{1,5},{5,1},{2,6},{6,2},{3,7},{7,3},{8,12},{12,8},{9,1... | collective-permute-start | bytes 1572872 | tf_op jit(solution)/shard_map/ppermute | solution.py:304
  50.0 4.6 %copy-start.4 = (s32[128]{0:T(128)S(1)}, s32[128]{0:T(128)}, u32[]{:S(2)}) copy-start(s32[128]{0:T(128)} %param.12) | copy-start | bytes 1540
  50.0 18.6 %all-to-all-start.1 = ((s16[4,128,896]{2,1,0:T(8,128)(2,1)}), s16[4,128,896]{2,1,0:T(8,128)(2,1)S(1)}, u32[]{:S(2)}, u32[]{:S(2)}) async-start(s16[4,128,896]{2,1,0:T(8,128)(2,1)} %shard_map.104), calls=%async_computation.1 | async-start | bytes 1835008 | tf_op jit(solution)/shard_map/all_to_all | solution.py:316
  85.2 4.7 %collective-permute-start.1 = (bf16[256,2304]{1,0:T(8,128)(2,1)S(1)}, bf16[256,2304]{1,0:T(8,128)(2,1)S(1)}, u32[]{:S(2)}, u32[]{:S(2)}) collective-permute-start(bf16[256,2304]{1,0:T(8,128)(2,1)S(1)} %shard_map.107), channel_id=1, source_target_pairs={{0,4},{4,0},{1,5},{5,1},{2,6},{6,2},{3,7},{7,3},{8,12},{12,8},{9,1... | collective-permute-start | bytes 3538952 | tf_op jit(solution)/shard_map/ppermute | solution.py:335
  111.1 6.1 %copy-start.7 = (s32[4]{0:T(128)S(1)}, s32[4]{0:T(128)}, u32[]{:S(2)}) copy-start(s32[4]{0:T(128)} %param.13) | copy-start | bytes 52
  111.1 6.2 %copy-start.5 = (f32[4]{0:T(128)S(1)}, f32[4]{0:T(128)}, u32[]{:S(2)}) copy-start(f32[4]{0:T(128)} %param.14) | copy-start | bytes 52
  111.1 6.3 %copy-start.6 = (f32[4]{0:T(128)S(1)}, f32[4]{0:T(128)}, u32[]{:S(2)}) copy-start(f32[4]{0:T(128)} %param.15) | copy-start | bytes 52
  111.1 25.0 %copy-start.3 = (bf16[4,1024]{1,0:T(4,128)(2,1)S(1)}, bf16[4,1024]{1,0:T(4,128)(2,1)}, u32[]{:S(2)}) copy-start(bf16[4,1024]{1,0:T(4,128)(2,1)} %hidden_ref.1) | copy-start | bytes 24580
  112.2 23.9 %all-to-all-start.3 = ((bf16[16,4,2432]{2,1,0:T(4,128)(2,1)}), bf16[16,4,2432]{2,1,0:T(4,128)(2,1)S(1)}, u32[]{:S(2)}, u32[]{:S(2)}) async-start(bf16[16,4,2432]{2,1,0:T(4,128)(2,1)} %shard_map.109), calls=%async_computation.3 | async-start | bytes 622592 | tf_op jit(solution)/shard_map/all_to_all | solution.py:341

commit v4 on v3

--- a/solution.py
+++ b/solution.py
@@ -10,7 +10,9 @@
 f32 = jnp.float32
 WIDTH = 1024
 VOCAB = 768
+PAIR = 2 * VOCAB
 FULL = 4096
+CODED = PAIR + 128
 STATS = 2 * WIDTH
 ROWS = STATS + 128
 NT = (((1,), (1,)), ((), ()))
@@ -70,106 +72,87 @@
     return (high + low / 16384.0) * unit_of(take(block, first, first + 1))
 
 
-def encode(ref, gain_ref, value_ref, head_ref):
-    rows = ref[...].astype(f32)
+def project(own_ref, gain_ref, value_ref, near_ref, far_ref, out_ref):
+    rows = own_ref[...].astype(f32)
     gained = rows * gain_ref[...]
     squares = jnp.sum(rows * rows, axis=1, keepdims=True)
     raw_values = jnp.sum(gained * value_ref[...], axis=1, keepdims=True)
     high = gained.astype(bf16)
     low = (gained - high.astype(f32)).astype(bf16)
-    logits = lax.dot_general(high, head_ref[...], NT, preferred_element_type=f32)
-    logits += lax.dot_general(low, head_ref[...], NT, preferred_element_type=f32)
-    exponent = exponent_of(jnp.max(jnp.abs(logits), axis=1, keepdims=True))
-    whole = jnp.round(logits * (1.0 / unit_of(exponent))).astype(jnp.int32).astype(jnp.int16)
-    block = lanes(256, [exponent] + digits(squares) + digits(raw_values))
-    return whole, block.astype(jnp.int32).astype(jnp.int16)
-
-
-def project_own(own_ref, gain_ref, value_ref, head_ref, out_ref):
-    out_ref[:, :VOCAB], out_ref[:, VOCAB:] = encode(own_ref, gain_ref, value_ref, head_ref)
-
-
-def project(first_ref, other_ref, gain_ref, value_ref, head_ref, out_ref):
-    whole, block = encode(other_ref, gain_ref, value_ref, head_ref)
-    for x in range(4):
-        for s in range(4):
-            source = slice(x * 64 + s * 16, x * 64 + s * 16 + 16)
-            out_ref[s, x * 16 : x * 16 + 16] = first_ref[source]
-            out_ref[s, 64 + x * 16 : 64 + x * 16 + 16, :VOCAB] = whole[source]
-            out_ref[s, 64 + x * 16 : 64 + x * 16 + 16, VOCAB:] = block[source]
+    logits = []
+    for ref in (near_ref, far_ref):
+        part = lax.dot_general(high, ref[...], NT, preferred_element_type=f32)
+        logits.append(part + lax.dot_general(low, ref[...], NT, preferred_element_type=f32))
+    largest = [jnp.max(jnp.abs(part), axis=1, keepdims=True) for part in logits]
+    exponent = exponent_of(jnp.maximum(*largest))
+    scale = 1.0 / unit_of(exponent)
+    pieces = [jnp.round(part * scale) for part in logits]
+    pieces.append(lanes(256, [exponent] + digits(squares) + digits(raw_values)))
+    for index, piece in enumerate(pieces):
+        piece = piece.astype(jnp.int32).astype(jnp.int16)
+        columns = slice(index * VOCAB, min((index + 1) * VOCAB, CODED))
+        for x in range(4):
+            for s in range(4):
+                source = slice(x * 64 + s * 16, x * 64 + s * 16 + 16)
+                out_ref[s, x * 16 : x * 16 + 16, columns] = piece[source]
 
 
 def soften(core_ref, parts_ref, wanted_ref, out_ref, rows_ref):
     squares = raw_values = logits = 0.0
     for source in range(4):
-        block = parts_ref[source, :, VOCAB:].astype(jnp.int32).astype(f32)
-        whole = parts_ref[source, :, :VOCAB].astype(jnp.int32).astype(f32)
+        block = parts_ref[source, :, PAIR:].astype(jnp.int32).astype(f32)
+        whole = parts_ref[source, :, :PAIR].astype(jnp.int32).astype(f32)
         logits = logits + whole * unit_of(take(block, 0, 1))
         squares = squares + undigits(block, 1)
         raw_values = raw_values + undigits(block, 4)
     inverse = lax.rsqrt(squares / FULL + epsilon)
     values = inverse * raw_values
     logits = logits * inverse
-    column = lax.broadcasted_iota(jnp.int32, (128, VOCAB), 1)
+    column = lax.broadcasted_iota(jnp.int32, (64, PAIR), 1)
     matches = column == wanted_ref[...]
     top = jnp.max(logits, axis=1, keepdims=True).astype(bf16).astype(f32)
     exps = jnp.exp(logits - top)
     total = jnp.sum(exps, axis=1, keepdims=True)
     first = jnp.sum(exps * logits, axis=1, keepdims=True)
     picked = jnp.sum(jnp.where(matches, logits, 0.0), axis=1, keepdims=True)
-    out_ref[:, :VOCAB] = jnp.where(matches, -1.0, exps).astype(bf16)
+    out_ref[:, :PAIR] = jnp.where(matches, -1.0, exps).astype(bf16)
     stats = [top] + two(total) + two(first) + two(picked) + three(inverse) + three(values)
-    out_ref[:, VOCAB:] = lanes(128, stats).astype(bf16)
-    pieces = lanes(128, [top] + two(total) + two(picked)).astype(bf16)
-    place = lax.broadcasted_iota(jnp.int32, (128, 128), 0)
-    natural = lax.broadcasted_iota(jnp.int32, (128, 128), 1)
-    wanted_place = (
-        ((natural // 16) % 2 ^ core_ref[0]) * 64
-        + ((natural // 4) % 4) * 16
-        + (natural // 32) * 4
-        + natural % 4
-    )
-    moved = jnp.where(place == wanted_place, 1.0, 0.0).astype(bf16)
+    out_ref[:, PAIR:] = lanes(64, stats).astype(bf16)
+    pieces = lanes(64, [top] + two(total) + two(picked)).astype(bf16)
+    place = lax.broadcasted_iota(jnp.int32, (64, 128), 0)
+    natural = lax.broadcasted_iota(jnp.int32, (64, 128), 1)
+    wanted_place = ((natural // 4) % 4) * 16 + (natural // 32) * 4 + natural % 4
+    mine = (natural // 16) % 2 == core_ref[0]
+    moved = jnp.where((place == wanted_place) & mine, 1.0, 0.0).astype(bf16)
     rows_ref[...] = lax.dot_general(
         pieces, moved, (((0,), (0,)), ((), ())), preferred_element_type=f32
     )[0:16].astype(bf16)
 
 
-def row_parts(top, total, picked):
-    pieces = [top] + two(total) + two(picked)
-    row = lax.broadcasted_iota(jnp.int32, (16, 128), 0)
-    block = jnp.zeros((16, 128), f32)
-    for index, piece in enumerate(pieces):
-        block = jnp.where(row == index, piece, block)
-    return block.astype(bf16)
-
-
-def pull(half, exps_ref, head_ref, out_ref):
+def pull(exps_ref, near_ref, far_ref, rows_ref, got_ref, out_ref):
     pieces = [
-        exps_ref[s, half * 64 + x * 16 : half * 64 + x * 16 + 16]
-        for x in range(4)
-        for s in range(4)
+        exps_ref[s, x * 16 : x * 16 + 16] for x in range(4) for s in range(4)
     ]
     chosen = jnp.concatenate(pieces, axis=0)
-    exps = chosen[:, :VOCAB].astype(f32)
-    head = head_ref[...]
-    out_ref[:, 0:WIDTH] = jnp.dot(
-        jnp.maximum(exps, 0.0).astype(bf16), head, preferred_element_type=f32
-    ).astype(bf16)
-    out_ref[:, WIDTH:STATS] = jnp.dot(
-        jnp.where(exps < 0.0, 1.0, 0.0).astype(bf16), head, preferred_element_type=f32
-    ).astype(bf16)
-    out_ref[:, STATS:ROWS] = chosen[:, VOCAB:]
-
-
-def pull_own(exps_ref, head_ref, out_ref):
-    pull(0, exps_ref, head_ref, out_ref)
-
-
-def pull_other(exps_ref, head_ref, rows_ref, out_ref):
-    pull(1, exps_ref, head_ref, out_ref)
-    out_ref[0:16, ROWS:] = rows_ref[...]
-    out_ref[16:, ROWS:] = jnp.zeros((240, 128), bf16)
+    product = wanted = 0.0
+    for index, ref in enumerate((near_ref, far_ref)):
+        exps = chosen[:, index * VOCAB : (index + 1) * VOCAB].astype(f32)
+        head = ref[...]
+        product += jnp.dot(
+            jnp.maximum(exps, 0.0).astype(bf16), head, preferred_element_type=f32
+        )
+        wanted += jnp.dot(
+            jnp.where(exps < 0.0, 1.0, 0.0).astype(bf16), head, preferred_element_type=f32
+        )
+    product, wanted = product.astype(bf16), wanted.astype(bf16)
+    rows = (rows_ref[...].astype(f32) + got_ref[...].astype(f32)).astype(bf16)
+    for x in range(4):
+        some = slice(x * 64, x * 64 + 64)
+        out_ref[x, :, 0:WIDTH] = product[some]
+        out_ref[x, :, WIDTH:STATS] = wanted[some]
+        out_ref[x, :, STATS:ROWS] = chosen[some, PAIR:]
+        out_ref[x, 0:16, ROWS:] = rows
+        out_ref[x, 16:64, ROWS:] = jnp.zeros((48, 128), bf16)
 
 
 def read_rows(block):
@@ -207,24 +190,6 @@
 def join_rows(blocks):
     top, _, total = merge(blocks)
     return top, total, sum(block[2] for block in blocks)
-
-
-def join_core(own_ref, got_ref, rows_ref, out_ref):
-    product, top, total, first, picked = join(
-        [(ref[:, 0:WIDTH], ref[:, STATS:ROWS]) for ref in (own_ref, got_ref)]
-    )
-    wanted = own_ref[:, WIDTH:STATS].astype(f32) + got_ref[:, WIDTH:STATS].astype(f32)
-    block = row_parts(
-        *join_rows([read_rows(rows_ref[...]), read_rows(got_ref[0:16, ROWS:])])
-    )
-    stats = lanes(256, [top] + two(total) + two(first) + two(picked)).astype(bf16)
-    product, wanted = product.astype(bf16), wanted.astype(bf16)
-    for x in range(4):
-        out_ref[x, :, 0:WIDTH] = product[x * 64 : x * 64 + 64]
-        out_ref[x, :, WIDTH:STATS] = wanted[x * 64 : x * 64 + 64]
-        out_ref[x, :, STATS:ROWS] = stats[x * 64 : x * 64 + 64]
-        out_ref[x, 0:16, ROWS:] = block
-        out_ref[x, 16:64, ROWS:] = jnp.zeros((48, 128), bf16)
 
 
 def join_x(got_ref, out_ref):
@@ -295,32 +260,34 @@
 ):
     core = lax.axis_index("core")
     z, x = lax.axis_index("z"), lax.axis_index("x")
-    shard = (z * 2 + core) * 4 + x
+    near = (z * 2 + core) * 4 + x
+    far = (z * 2 + 1 - core) * 4 + x
     gain, value_row = norm_gain[None, :], value_weight[None, :]
     swap = [(0, 1), (1, 0)]
 
+    far_weight = lax.ppermute(head_weight, "core", swap)
     by_z = spread(hidden, "z")
-    own = lax.all_gather(by_z, "x", axis=0).reshape(256, WIDTH)
-    other = lax.ppermute(own, "core", swap)
-    coded = (256, VOCAB + 128)
-    (first,) = call(project_own, [(coded, jnp.int16)], own, gain, value_row, head_weight)
+    own = lax.all_gather(by_z.reshape(64, WIDTH), "x", axis=0, tiled=True)
     (sent,) = call(
         project,
-        [((4, 128, VOCAB + 128), jnp.int16)],
-        first,
-        other,
+        [((4, 64, CODED), jnp.int16)],
+        own,
         gain,
         value_row,
         head_weight,
+        far_weight,
     )
     parts = lax.all_to_all(sent, "section", 0, 0)
 
-    block = targets.reshape(4, 2, 4, 4).transpose(1, 2, 0, 3)
-    block = jnp.where(core == 0, block, block[::-1]).reshape(128, 1) - shard * VOCAB
+    block = targets.reshape(4, 2, 4, 4).transpose(1, 2, 0, 3).reshape(2, 64)
+    block = jnp.where(core == 0, block[0], block[1])
+    in_near, in_far = block - near * VOCAB, block - far * VOCAB
+    place = jnp.where((in_near >= 0) & (in_near < VOCAB), in_near, -1)
+    place = jnp.where((in_far >= 0) & (in_far < VOCAB), in_far + VOCAB, place)
     exps, rows = pl.pallas_call(
         soften,
         out_shape=[
-            jax.ShapeDtypeStruct((128, VOCAB + 128), bf16),
+            jax.ShapeDtypeStruct((64, CODED), bf16),
             jax.ShapeDtypeStruct((16, 128), bf16),
         ],
         in_specs=[
@@ -329,13 +296,19 @@
             pl.BlockSpec(memory_space=pltpu.VMEM),
         ],
         compiler_params=pltpu.CompilerParams(vmem_limit_bytes=SCOPED),
-    )(core.astype(jnp.int32).reshape(1), parts, block)
+    )(core.astype(jnp.int32).reshape(1), parts, place.reshape(64, 1))
+    got_rows = lax.ppermute(rows, "core", swap)
     every = lax.all_gather(exps, "section", axis=0)
-    (theirs,) = call(pull_other, [((256, ROWS + 128), bf16)], every, head_weight, rows)
-    got = lax.ppermute(theirs, "core", swap)
-    (mine,) = call(pull_own, [((256, ROWS), bf16)], every, head_weight)
-    own_stats = lax.dynamic_slice(mine, (x * 64 + z * 4, STATS), (4, 128))
-    (sent,) = call(join_core, [((4, 64, 2 * WIDTH + 256), bf16)], mine, got, rows)
+    (sent,) = call(
+        pull,
+        [((4, 64, ROWS + 128), bf16)],
+        every,
+        head_weight,
+        far_weight,
+        rows,
+        got_rows,
+    )
+    own_stats = lax.dynamic_slice(every, (z // 4, x * 16 + (z % 4) * 4, PAIR), (1, 4, 128))[0]
     got = lax.all_to_all(sent, "x", 0, 0)
     (sent,) = call(join_x, [((16, 4, 2 * WIDTH + 384), bf16)], got)
     got = lax.all_to_all(sent, "z", 0, 0)

time: 137 us -> 132 us (0.964)
  blocking collectives: 77.3 us -> 46.3 us
  starting transfers between devices: 13.4 us -> 28.7 us
  waiting for transfers between devices: 34 us -> 40 us
  local copies, waits for them, and re-layouts: 1.49 us -> 7.17 us
    all_to_all x1 -> x0, blocking collectives: 29.2 us -> none  [spread(): return lax.all_to_all(copies, axis, 0, 0)]
    all_to_all x0 -> x1, starting transfers between devices: none -> 15.2 us  [spread(): return lax.all_to_all(copies, axis, 0, 0)]
    all_to_all x0 -> x1, waiting for transfers between devices: none -> 13.7 us  [spread(): return lax.all_to_all(copies, axis, 0, 0)]
    all_to_all x1, waiting for transfers between devices: 13.7 us -> 9.77 us  [shards(): parts = lax.all_to_all(sent, 'section', 0, 0)]
    unnamed x16 -> x24, local copies, waits for them, and re-layouts: 0.03 us -> 3.76 us
    ppermute x2, waiting for transfers between devices: 2.43 us -> 0.01 us  [the longest x1 0.01 us: shards(): got_rows = lax.ppermute(rows, 'core', swap)]
    pallas_call x7 -> x4, Pallas kernels: 8.24 us -> 5.95 us  [call(): pl.pallas_call(body, out_shape=[jax.ShapeDtypeStruct(shape, dtype) for sh...]
    all_to_all x1, blocking collectives: 20.3 us -> 18.3 us  [shards(): got = lax.all_to_all(sent, 'x', 0, 0)]
  transfers between devices with their start and end apart: 4 -> 5, of which waited for: 4 -> 3; matrix products, arithmetic and copies ran while one was open for 1% -> 3% of each run, Pallas kernels for 2% -> 0%
where the time goes in v4:
time: 132 us
  blocking collectives  46.3 us (35%)
  waiting for transfers between devices  40 us (30%)
  starting transfers between devices  28.7 us (22%)
  Pallas kernels  7.88 us (6%)
  local copies, waits for them, and re-layouts  7.17 us (5%)
    all_to_all x1, blocking collectives, shards(): got = lax.all_to_all(sent, 'x', 0, 0)  18.3 us
    all_to_all x1, waiting for transfers between devices, shards(): got = lax.all_to_all(sent, 'z', 0, 0)  16.5 us
    all_to_all x1, starting transfers between devices, spread(): return lax.all_to_all(copies, axis, 0, 0)  15.2 us
    all_gather x1, blocking collectives, shards(): every = lax.all_gather(exps, 'section', axis=0)  14.6 us
    all_to_all x1, waiting for transfers between devices, spread(): return lax.all_to_all(copies, axis, 0, 0)  13.7 us
    all_gather x1, blocking collectives, shards(): own = lax.all_gather(by_z.reshape(64, WIDTH), 'x', axis=0, tiled=True)  13.4 us
    all_to_all x1, waiting for transfers between devices, shards(): parts = lax.all_to_all(sent, 'section', 0, 0)  9.77 us
    pallas_call x4, Pallas kernels, call(): pl.pallas_call(body, out_shape=[jax.ShapeDtypeStruct(shape, dtype) for sh...  5.95 us
  transfers between devices with their start and end apart: 5, of which 3 were waited for; matrix products, arithmetic and copies ran while one was open for 3% of the time, Pallas kernels for 0%

profile of v4, /device:TPU:32, one launch (start us, length us, event | category | flops | bytes accessed | tf_op | source)
XLA Modules:
  0.0 131.6 jit_solution(10903580582941376549)
XLA Ops:
  0.6 1.9 %collective-permute-start = (bf16[768,1024]{1,0:T(8,128)(2,1)}, bf16[768,1024]{1,0:T(8,128)(2,1)S(1)}, u32[]{:S(2)}, u32[]{:S(2)}) collective-permute-start(bf16[768,1024]{1,0:T(8,128)(2,1)} %near_ref.3), channel_id=1, source_target_pairs={{0,4},{4,0},{1,5},{5,1},{2,6},{6,2},{3,7},{7,3},{8,12},{12,8},{9,1... | collective-permute-start | bytes 4718600 | tf_op jit(solution)/shard_map/ppermute | solution.py:268
  2.6 1.4 %broadcast_in_dim.16 = bf16[16,4,1024]{2,1,0:T(4,128)(2,1)} broadcast(bf16[4,1024]{1,0:T(4,128)(2,1)} %hidden_ref.1), dimensions={1,2} | broadcast | bytes 139264 | tf_op jit(solution)/shard_map/broadcast_in_dim | solution.py:254
  3.9 15.2 %all-to-all-start = ((bf16[16,4,1024]{2,1,0:T(4,128)(2,1)}), bf16[16,4,1024]{2,1,0:T(4,128)(2,1)S(1)}, u32[]{:S(2)}, u32[]{:S(2)}) async-start(bf16[16,4,1024]{2,1,0:T(4,128)(2,1)} %broadcast_in_dim.16), calls=%async_computation | async-start | bytes 262144 | tf_op jit(solution)/shard_map/all_to_all | solution.py:255
  19.2 0.8 reshape.90
  20.0 13.7 %all-to-all-done = bf16[16,4,1024]{2,1,0:T(4,128)(2,1)S(1)} async-done(((bf16[16,4,1024]{2,1,0:T(4,128)(2,1)}), bf16[16,4,1024]{2,1,0:T(4,128)(2,1)S(1)}, u32[]{:S(2)}, u32[]{:S(2)}) %all-to-all-start) | async-done | bytes 131104 | tf_op jit(solution)/shard_map/all_to_all | solution.py:255
  33.7 13.4 %all_gather.9.own_ref = bf16[256,1024]{1,0:T(8,128)(2,1)S(1)} all-gather(bf16[64,1024]{1,0:T(8,128)(2,1)S(1)} %reshape.89), channel_id=1, replica_groups=mesh['section'=4,'z'=16,'core'=2,'x'=4] {'x'}, dimensions={0}, use_global_device_ids=true | all-gather | bytes 655360 | tf_op jit(solution)/shard_map/all_gather | solution.py:270
  47.1 0.0 collective-permute-done.far_ref
  47.1 0.0 copy-start
  47.1 1.4 %copy-done = bf16[768,1024]{1,0:T(8,128)(2,1)S(1)} copy-done((bf16[768,1024]{1,0:T(8,128)(2,1)S(1)}, bf16[768,1024]{1,0:T(8,128)(2,1)}, u32[]{:S(2)}) %copy-start) | copy-done | bytes 1572888
  48.5 0.0 copy-start.5
  48.5 0.7 copy-done.5
  49.2 0.0 copy-start.7
  49.2 0.7 copy-done.7
  49.9 2.1 %shard_map.103 = s16[4,64,1664]{2,1,0:T(8,128)(2,1)S(1)} custom-call(bf16[256,1024]{1,0:T(8,128)(2,1)S(1)} %all_gather.9.own_ref, f32[1,1024]{1,0:T(1,128)S(1)} %bitcast.14, f32[1,1024]{1,0:T(1,128)S(1)} %bitcast.16, bf16[768,1024]{1,0:T(8,128)(2,1)S(1)} %copy-done, bf16[768,1024]{1,0:T(8,128)(2,1)S(1)} %collective-permute-done.far_ref), custom_call_target="tpu_custom_call" | custom-call | tf_op jit(solution)/shard_map/pallas_call | solution.py:47
  52.0 0.0 copy-start.3
  52.0 0.9 copy-done.3
  52.9 0.0 copy-start.1
  52.9 4.6 %all-to-all-start.1 = ((s16[4,64,1664]{2,1,0:T(8,128)(2,1)}), s16[4,64,1664]{2,1,0:T(8,128)(2,1)}, u32[]{:S(2)}, u32[]{:S(2)}) async-start(s16[4,64,1664]{2,1,0:T(8,128)(2,1)} %copy-done.3), calls=%async_computation.1 | async-start | bytes 1703936 | tf_op jit(solution)/shard_map/all_to_all | solution.py:280
  57.5 0.1 add.49
  57.7 0.1 and.41
  57.7 0.1 sub.44
  57.8 9.8 %all-to-all-done.1.parts_ref = s16[4,64,1664]{2,1,0:T(8,128)(2,1)} async-done(((s16[4,64,1664]{2,1,0:T(8,128)(2,1)}), s16[4,64,1664]{2,1,0:T(8,128)(2,1)}, u32[]{:S(2)}, u32[]{:S(2)}) %all-to-all-start.1) | async-done | bytes 852000 | tf_op jit(solution)/shard_map/all_to_all | solution.py:280
  67.6 1.9 %shard_map.104 = (bf16[64,1664]{1,0:T(8,128)(2,1)S(1)}, bf16[16,128]{1,0:T(8,128)(2,1)S(1)}) custom-call(s32[1]{0:T(128)} %bitcast.core_ref, s16[4,64,1664]{2,1,0:T(8,128)(2,1)} %all-to-all-done.1.parts_ref, s32[64,1]{1,0:T(8,128)S(1)} %select_select_fusion.wanted_ref), custom_call_target="tpu_custom_call" | custom-call | tf_op jit(solution)/shard_map/pallas_call | solution.py:287
  69.5 1.9 %collective-permute-start.1 = (bf16[16,128]{1,0:T(8,128)(2,1)S(1)}, bf16[16,128]{1,0:T(8,128)(2,1)S(1)}, u32[]{:S(2)}, u32[]{:S(2)}) collective-permute-start(bf16[16,128]{1,0:T(8,128)(2,1)S(1)} %get-tuple-element.8.rows_ref), channel_id=1, source_target_pairs={{0,4},{4,0},{1,5},{5,1},{2,6},{6,2},{3,7},{7,3},{8,12},{12,8},{9,1... | collective-permute-start | bytes 12296 | tf_op jit(solution)/shard_map/ppermute | solution.py:300
  71.5 14.6 %all-gather = bf16[256,1664]{1,0:T(8,128)(2,1)S(1)} all-gather(bf16[64,1664]{1,0:T(8,128)(2,1)S(1)} %get-tuple-element.7), channel_id=2, replica_groups=mesh['section'=4,'z'=16,'core'=2,'x'=4] {'section'}, dimensions={0}, use_global_device_ids=true | all-gather | bytes 1064960 | tf_op jit(solution)/shard_map/all_gather | solution.py:301
  86.0 0.0 collective-permute-done.1.got_ref
  86.0 0.0 copy-done.1
  86.1 1.8 %shard_map.105 = bf16[4,64,2304]{2,1,0:T(8,128)(2,1)S(1)} custom-call(bf16[4,64,1664]{2,1,0:T(8,128)(2,1)S(1)} %bitcast.12, bf16[768,1024]{1,0:T(8,128)(2,1)S(1)} %copy-done.1, bf16[768,1024]{1,0:T(8,128)(2,1)S(1)} %collective-permute-done.far_ref, bf16[16,128]{1,0:T(8,128)(2,1)S(1)} %get-tuple-element.8.rows_ref, ...), custom_call_target="tpu_custom_call" | custom-call | tf_op jit(solution)/shard_map/pallas_call | solution.py:47
  87.8 0.0 copy-done.2
  87.9 18.3 %all_to_all.20.got_ref = bf16[4,64,2304]{2,1,0:T(8,128)(2,1)S(1)} all-to-all(bf16[4,64,2304]{2,1,0:T(8,128)(2,1)S(1)} %shard_map.105), channel_id=1, replica_groups=mesh['section'=4,'z'=16,'core'=2,'x'=4] {'x'}, dimensions={0} | all-to-all | bytes 2359296 | tf_op jit(solution)/shard_map/all_to_all | solution.py:312
  106.2 0.0 copy-start.6
  106.2 0.0 copy-start.8
  106.2 1.1 shard_map.106
  107.3 5.0 %all-to-all-start.3 = ((bf16[16,4,2432]{2,1,0:T(4,128)(2,1)}), bf16[16,4,2432]{2,1,0:T(4,128)(2,1)S(1)}, u32[]{:S(2)}, u32[]{:S(2)}) async-start(bf16[16,4,2432]{2,1,0:T(4,128)(2,1)} %shard_map.106), calls=%async_computation.3 | async-start | bytes 622592 | tf_op jit(solution)/shard_map/all_to_all | solution.py:314
  112.4 0.0 copy-done.11
  112.4 0.1 copy.19
  112.5 0.0 copy-done.9
  112.5 0.1 copy.20
  112.6 0.0 copy-done.10
  112.6 0.1 copy.21
  112.7 0.1 pad_maximum_fusion.token_ref
  112.8 0.7 dynamic-slice_bitcast_fusion.own_ref
  113.5 0.7 convert_reduce_fusion
  114.2 16.5 %all-to-all-done.3.got_ref = bf16[16,4,2432]{2,1,0:T(4,128)(2,1)S(1)} async-done(((bf16[16,4,2432]{2,1,0:T(4,128)(2,1)}), bf16[16,4,2432]{2,1,0:T(4,128)(2,1)S(1)}, u32[]{:S(2)}, u32[]{:S(2)}) %all-to-all-start.3) | async-done | bytes 311328 | tf_op jit(solution)/shard_map/all_to_all | solution.py:314
  130.7 0.0 copy-done.4
  130.7 0.0 copy-done.6
  130.7 0.0 copy-done.8
  130.7 0.9 shard_map.107
  (14 shorter events, 0.1 us)
Async XLA Ops:
  0.6 46.5 %collective-permute-start = (bf16[768,1024]{1,0:T(8,128)(2,1)}, bf16[768,1024]{1,0:T(8,128)(2,1)S(1)}, u32[]{:S(2)}, u32[]{:S(2)}) collective-permute-start(bf16[768,1024]{1,0:T(8,128)(2,1)} %near_ref.3), channel_id=1, source_target_pairs={{0,4},{4,0},{1,5},{5,1},{2,6},{6,2},{3,7},{7,3},{8,12},{12,8},{9,1... | collective-permute-start | bytes 4718600 | tf_op jit(solution)/shard_map/ppermute | solution.py:268
  3.9 29.7 %all-to-all-start = ((bf16[16,4,1024]{2,1,0:T(4,128)(2,1)}), bf16[16,4,1024]{2,1,0:T(4,128)(2,1)S(1)}, u32[]{:S(2)}, u32[]{:S(2)}) async-start(bf16[16,4,1024]{2,1,0:T(4,128)(2,1)} %broadcast_in_dim.16), calls=%async_computation | async-start | bytes 262144 | tf_op jit(solution)/shard_map/all_to_all | solution.py:255
  47.1 1.4 %copy-start = (bf16[768,1024]{1,0:T(8,128)(2,1)S(1)}, bf16[768,1024]{1,0:T(8,128)(2,1)}, u32[]{:S(2)}) copy-start(bf16[768,1024]{1,0:T(8,128)(2,1)} %near_ref.3) | copy-start | bytes 4718596
  48.5 0.7 copy-start.5
  49.2 0.7 copy-start.7
  52.0 1.0 copy-start.3
  52.9 33.1 %copy-start.1 = (bf16[768,1024]{1,0:T(8,128)(2,1)S(1)}, bf16[768,1024]{1,0:T(8,128)(2,1)}, u32[]{:S(2)}) copy-start(bf16[768,1024]{1,0:T(8,128)(2,1)} %near_ref.3) | copy-start | bytes 4718596
  52.9 14.7 %all-to-all-start.1 = ((s16[4,64,1664]{2,1,0:T(8,128)(2,1)}), s16[4,64,1664]{2,1,0:T(8,128)(2,1)}, u32[]{:S(2)}, u32[]{:S(2)}) async-start(s16[4,64,1664]{2,1,0:T(8,128)(2,1)} %copy-done.3), calls=%async_computation.1 | async-start | bytes 1703936 | tf_op jit(solution)/shard_map/all_to_all | solution.py:280
  69.5 16.5 %collective-permute-start.1 = (bf16[16,128]{1,0:T(8,128)(2,1)S(1)}, bf16[16,128]{1,0:T(8,128)(2,1)S(1)}, u32[]{:S(2)}, u32[]{:S(2)}) collective-permute-start(bf16[16,128]{1,0:T(8,128)(2,1)S(1)} %get-tuple-element.8.rows_ref), channel_id=1, source_target_pairs={{0,4},{4,0},{1,5},{5,1},{2,6},{6,2},{3,7},{7,3},{8,12},{12,8},{9,1... | collective-permute-start | bytes 12296 | tf_op jit(solution)/shard_map/ppermute | solution.py:300
  86.0 1.8 %copy-start.2 = (bf16[256,1664]{1,0:T(8,128)(2,1)}, bf16[256,1664]{1,0:T(8,128)(2,1)S(1)}, u32[]{:S(2)}) copy-start(bf16[256,1664]{1,0:T(8,128)(2,1)S(1)} %all-gather) | copy-start | bytes 2555908
  106.2 6.2 %copy-start.11 = (s32[4]{0:T(128)S(1)}, s32[4]{0:T(128)}, u32[]{:S(2)}) copy-start(s32[4]{0:T(128)} %param.13) | copy-start | bytes 52
  106.2 6.3 %copy-start.9 = (f32[4]{0:T(128)S(1)}, f32[4]{0:T(128)}, u32[]{:S(2)}) copy-start(f32[4]{0:T(128)} %param.14) | copy-start | bytes 52
  106.2 6.4 %copy-start.10 = (f32[4]{0:T(128)S(1)}, f32[4]{0:T(128)}, u32[]{:S(2)}) copy-start(f32[4]{0:T(128)} %param.15) | copy-start | bytes 52
  106.2 24.5 %copy-start.4 = (bf16[4,1024]{1,0:T(4,128)(2,1)S(1)}, bf16[4,1024]{1,0:T(4,128)(2,1)}, u32[]{:S(2)}) copy-start(bf16[4,1024]{1,0:T(4,128)(2,1)} %hidden_ref.1) | copy-start | bytes 24580
  106.2 24.5 %copy-start.6 = (f32[1024]{0:T(1024)S(1)}, f32[1024]{0:T(1024)}, u32[]{:S(2)}) copy-start(f32[1024]{0:T(1024)} %param.9) | copy-start | bytes 12292
  106.2 24.5 %copy-start.8 = (f32[1024]{0:T(1024)S(1)}, f32[1024]{0:T(1024)}, u32[]{:S(2)}) copy-start(f32[1024]{0:T(1024)} %param.10) | copy-start | bytes 12292
  107.3 23.3 %all-to-all-start.3 = ((bf16[16,4,2432]{2,1,0:T(4,128)(2,1)}), bf16[16,4,2432]{2,1,0:T(4,128)(2,1)S(1)}, u32[]{:S(2)}, u32[]{:S(2)}) async-start(bf16[16,4,2432]{2,1,0:T(4,128)(2,1)} %shard_map.106), calls=%async_computation.3 | async-start | bytes 622592 | tf_op jit(solution)/shard_map/all_to_all | solution.py:314

commit v5 on v4

--- a/solution.py
+++ b/solution.py
@@ -11,6 +11,8 @@
 WIDTH = 1024
 VOCAB = 768
 PAIR = 2 * VOCAB
+PIECES = 4
+PARKED = 18432
 FULL = 4096
 CODED = PAIR + 128
 STATS = 2 * WIDTH
@@ -43,11 +45,18 @@
     return jnp.sum(kept, axis=-1, keepdims=True)
 
 
-def call(body, outs, *args, scratch=()):
+def call(body, outs, *args, parked=None):
+    scratch = []
+    if parked is not None:
+        scratch = [pltpu.VMEM((VOCAB, WIDTH), bf16), pltpu.SemaphoreType.DMA((PIECES,))]
     return pl.pallas_call(
         body,
         out_shape=[jax.ShapeDtypeStruct(shape, dtype) for shape, dtype in outs],
-        scratch_shapes=list(scratch),
+        in_specs=[
+            pl.BlockSpec(memory_space=pl.ANY if index == parked else pltpu.VMEM)
+            for index in range(len(args))
+        ],
+        scratch_shapes=scratch,
         compiler_params=pltpu.CompilerParams(vmem_limit_bytes=SCOPED),
     )(*args)
 
@@ -72,7 +81,25 @@
     return (high + low / 16384.0) * unit_of(take(block, first, first + 1))
 
 
-def project(own_ref, gain_ref, value_ref, near_ref, far_ref, out_ref):
+def pieces_of(source, target, arrived):
+    copies = []
+    for index in range(PIECES):
+        rows = pl.ds(index * (VOCAB // PIECES), VOCAB // PIECES)
+        copies.append(
+            pltpu.make_async_copy(source.at[rows], target.at[rows], arrived.at[index])
+        )
+    for copy in copies:
+        copy.start()
+    return copies
+
+
+def park(far_ref, out_ref, arrived):
+    for copy in pieces_of(far_ref, out_ref, arrived):
+        copy.wait()
+
+
+def project(own_ref, gain_ref, value_ref, near_ref, far_ref, out_ref, far_held, arrived):
+    copies = pieces_of(far_ref, far_held, arrived)
     rows = own_ref[...].astype(f32)
     gained = rows * gain_ref[...]
     squares = jnp.sum(rows * rows, axis=1, keepdims=True)
@@ -80,7 +107,10 @@
     high = gained.astype(bf16)
     low = (gained - high.astype(f32)).astype(bf16)
     logits = []
-    for ref in (near_ref, far_ref):
+    for ref in (near_ref, far_held):
+        if ref is far_held:
+            for copy in copies:
+                copy.wait()
         part = lax.dot_general(high, ref[...], NT, preferred_element_type=f32)
         logits.append(part + lax.dot_general(low, ref[...], NT, preferred_element_type=f32))
     largest = [jnp.max(jnp.abs(part), axis=1, keepdims=True) for part in logits]
@@ -129,13 +159,17 @@
     )[0:16].astype(bf16)
 
 
-def pull(exps_ref, near_ref, far_ref, rows_ref, got_ref, out_ref):
+def pull(exps_ref, near_ref, far_ref, rows_ref, got_ref, out_ref, far_held, arrived):
+    copies = pieces_of(far_ref, far_held, arrived)
     pieces = [
         exps_ref[s, x * 16 : x * 16 + 16] for x in range(4) for s in range(4)
     ]
     chosen = jnp.concatenate(pieces, axis=0)
     product = wanted = 0.0
-    for index, ref in enumerate((near_ref, far_ref)):
+    for index, ref in enumerate((near_ref, far_held)):
+        if ref is far_held:
+            for copy in copies:
+                copy.wait()
         exps = chosen[:, index * VOCAB : (index + 1) * VOCAB].astype(f32)
         head = ref[...]
         product += jnp.dot(
@@ -200,20 +234,18 @@
         [read_rows(got_ref[k, 0:16, ROWS:]) for k in range(4)]
     )
     stats = lanes(64, [top] + two(total) + two(first) + two(picked))
-    pieces = [top_row] + two(total_row) + two(picked_row)
+    pieces = two(top_row + jnp.log(total_row)) + two(picked_row)
     row = lax.broadcasted_iota(jnp.int32, (4, 128), 0)
-    left = jnp.zeros((4, 128), f32)
+    block = jnp.zeros((4, 128), f32)
     for index in range(4):
-        left = jnp.where(row == index, pieces[index], left)
-    right = jnp.where(row == 0, pieces[4], 0.0)
+        block = jnp.where(row == index, pieces[index], block)
     wanted = sum(got_ref[k, :, WIDTH:STATS].astype(f32) for k in range(4))
     for z in range(16):
         some = slice(z * 4, z * 4 + 4)
         out_ref[z, :, 0:WIDTH] = product[some].astype(bf16)
         out_ref[z, :, WIDTH : 2 * WIDTH] = wanted[some].astype(bf16)
         out_ref[z, :, 2 * WIDTH : 2 * WIDTH + 128] = stats[some].astype(bf16)
-        out_ref[z, :, 2 * WIDTH + 128 : 2 * WIDTH + 256] = left.astype(bf16)
-        out_ref[z, :, 2 * WIDTH + 256 :] = right.astype(bf16)
+        out_ref[z, :, ROWS:] = block.astype(bf16)
 
 
 def finish(
@@ -242,9 +274,8 @@
     ).astype(bf16)
     blocks = []
     for k in range(16):
-        left = got_ref[k, :, 2 * WIDTH + 128 : 2 * WIDTH + 256].astype(f32)
-        right = got_ref[k, :, 2 * WIDTH + 256 :].astype(f32)
-        blocks.append((left[0:1], left[1:2] + left[2:3], left[3:4] + right[0:1]))
+        block = got_ref[k, :, ROWS:].astype(f32)
+        blocks.append((block[0:1] + block[1:2], 1.0, block[2:3] + block[3:4]))
     top_row, total_row, picked_row = join_rows(blocks)
     logprobs_ref[...] = picked_row - (top_row + jnp.log(total_row))
 
@@ -266,7 +297,16 @@
     swap = [(0, 1), (1, 0)]
 
     far_weight = lax.ppermute(head_weight, "core", swap)
+    far_weight = pl.pallas_call(
+        park,
+        out_shape=jax.ShapeDtypeStruct((PARKED, WIDTH), bf16),
+        in_specs=[pl.BlockSpec(memory_space=pltpu.VMEM)],
+        out_specs=pl.BlockSpec(memory_space=pl.ANY),
+        scratch_shapes=[pltpu.SemaphoreType.DMA((PIECES,))],
+        compiler_params=pltpu.CompilerParams(vmem_limit_bytes=SCOPED),
+    )(far_weight)
     by_z = spread(hidden, "z")
+    by_z, far_weight = lax.optimization_barrier((by_z, far_weight))
     own = lax.all_gather(by_z.reshape(64, WIDTH), "x", axis=0, tiled=True)
     (sent,) = call(
         project,
@@ -276,6 +316,7 @@
         value_row,
         head_weight,
         far_weight,
+        parked=4,
     )
     parts = lax.all_to_all(sent, "section", 0, 0)
 
@@ -307,10 +348,11 @@
         far_weight,
         rows,
         got_rows,
+        parked=2,
     )
     own_stats = lax.dynamic_slice(every, (z // 4, x * 16 + (z % 4) * 4, PAIR), (1, 4, 128))[0]
     got = lax.all_to_all(sent, "x", 0, 0)
-    (sent,) = call(join_x, [((16, 4, 2 * WIDTH + 384), bf16)], got)
+    (sent,) = call(join_x, [((16, 4, ROWS + 128), bf16)], got)
     got = lax.all_to_all(sent, "z", 0, 0)
     token = jnp.stack([response_mask.astype(f32), loss_weight, value_target], axis=1)
     grad, logprobs = call(

time: 132 us -> 131 us (level)
  local copies, waits for them, and re-layouts: 7.17 us -> 2.74 us
  Pallas kernels: 7.88 us -> 12.3 us
  waiting for transfers between devices: 40 us -> 38.6 us
    pallas_call x4, Pallas kernels: 5.95 us -> 10.3 us  [call(): pl.pallas_call(body, out_shape=[jax.ShapeDtypeStruct(shape, dtype) for sh...]
    unnamed x24 -> x14, local copies, waits for them, and re-layouts: 3.76 us -> 0.03 us
  transfers between devices with their start and end apart: 5 -> 5, of which waited for: 3 -> 3; matrix products, arithmetic and copies ran while one was open for 3% -> 3% of each run, Pallas kernels for 0% -> 1%
where the time goes in v5:
time: 131 us; the launch traced here: 130 us
  blocking collectives  46.3 us (35%)
  waiting for transfers between devices  38.6 us (29%)
  starting transfers between devices  28.6 us (22%)
  Pallas kernels  12.3 us (9%)
  local copies, waits for them, and re-layouts  2.74 us (2%)
    all_to_all x1, blocking collectives, shards(): got = lax.all_to_all(sent, 'x', 0, 0)  18.3 us
    all_to_all x1, waiting for transfers between devices, shards(): got = lax.all_to_all(sent, 'z', 0, 0)  16.5 us
    all_to_all x1, starting transfers between devices, spread(): return lax.all_to_all(copies, axis, 0, 0)  15.2 us
    all_gather x1, blocking collectives, shards(): every = lax.all_gather(exps, 'section', axis=0)  14.6 us
    all_gather x1, blocking collectives, shards(): own = lax.all_gather(by_z.reshape(64, WIDTH), 'x', axis=0, tiled=True)  13.4 us
    all_to_all x1, waiting for transfers between devices, spread(): return lax.all_to_all(copies, axis, 0, 0)  12.4 us
    pallas_call x4, Pallas kernels, call(): pl.pallas_call(body, out_shape=[jax.ShapeDtypeStruct(shape, dtype) for sh...  10.3 us
    all_to_all x1, waiting for transfers between devices, shards(): parts = lax.all_to_all(sent, 'section', 0, 0)  9.65 us
  transfers between devices with their start and end apart: 5, of which 3 were waited for; matrix products, arithmetic and copies ran while one was open for 3% of the time, Pallas kernels for 1%

profile of v5, /device:TPU:32, one launch (start us, length us, event | category | flops | bytes accessed | tf_op | source)
XLA Modules:
  0.0 130.1 jit_solution(17958278577007145121)
XLA Ops:
  0.6 1.9 %collective-permute-start = (bf16[768,1024]{1,0:T(8,128)(2,1)}, bf16[768,1024]{1,0:T(8,128)(2,1)S(1)}, u32[]{:S(2)}, u32[]{:S(2)}) collective-permute-start(bf16[768,1024]{1,0:T(8,128)(2,1)} %near_ref.3), channel_id=1, source_target_pairs={{0,4},{4,0},{1,5},{5,1},{2,6},{6,2},{3,7},{7,3},{8,12},{12,8},{9,1... | collective-permute-start | bytes 4718600 | tf_op jit(solution)/shard_map/ppermute | solution.py:299
  2.6 1.4 %broadcast_in_dim.16 = bf16[16,4,1024]{2,1,0:T(4,128)(2,1)} broadcast(bf16[4,1024]{1,0:T(4,128)(2,1)} %hidden_ref.1), dimensions={1,2} | broadcast | bytes 139264 | tf_op jit(solution)/shard_map/broadcast_in_dim | solution.py:285
  3.9 15.2 %all-to-all-start = ((bf16[16,4,1024]{2,1,0:T(4,128)(2,1)}), bf16[16,4,1024]{2,1,0:T(4,128)(2,1)S(1)}, u32[]{:S(2)}, u32[]{:S(2)}) async-start(bf16[16,4,1024]{2,1,0:T(4,128)(2,1)} %broadcast_in_dim.16), calls=%async_computation | async-start | bytes 262144 | tf_op jit(solution)/shard_map/all_to_all | solution.py:286
  19.1 0.8 reshape.90
  19.9 0.0 copy-start.2
  20.0 0.0 copy-start.3
  20.0 0.0 collective-permute-done.far_ref
  20.0 0.0 copy-start
  20.0 1.2 shard_map.103.far_ref
  21.2 12.4 %all-to-all-done = bf16[16,4,1024]{2,1,0:T(4,128)(2,1)S(1)} async-done(((bf16[16,4,1024]{2,1,0:T(4,128)(2,1)}), bf16[16,4,1024]{2,1,0:T(4,128)(2,1)S(1)}, u32[]{:S(2)}, u32[]{:S(2)}) %all-to-all-start) | async-done | bytes 131104 | tf_op jit(solution)/shard_map/all_to_all | solution.py:286
  33.7 13.4 %all_gather.9.own_ref = bf16[256,1024]{1,0:T(8,128)(2,1)S(1)} all-gather(bf16[64,1024]{1,0:T(8,128)(2,1)S(1)} %reshape.89), channel_id=1, replica_groups=mesh['section'=4,'z'=16,'core'=2,'x'=4] {'x'}, dimensions={0}, use_global_device_ids=true | all-gather | bytes 655360 | tf_op jit(solution)/shard_map/all_gather | solution.py:310
  47.1 0.0 copy-done.2
  47.1 0.0 copy-done.3
  47.1 0.0 copy-done
  47.1 5.1 %shard_map.104 = s16[4,64,1664]{2,1,0:T(8,128)(2,1)} custom-call(bf16[256,1024]{1,0:T(8,128)(2,1)S(1)} %all_gather.9.own_ref, f32[1,1024]{1,0:T(1,128)S(1)} %bitcast.14, f32[1,1024]{1,0:T(1,128)S(1)} %bitcast.16, bf16[768,1024]{1,0:T(8,128)(2,1)S(1)} %copy-done, bf16[18432,1024]{1,0:T(8,128)(2,1)} %shard_map.103.far_ref), custom_call_target="tpu_custom_call" | custom-call | tf_op jit(solution)/shard_map/pallas_call | solution.py:52
  52.2 4.5 %all-to-all-start.1 = ((s16[4,64,1664]{2,1,0:T(8,128)(2,1)}), s16[4,64,1664]{2,1,0:T(8,128)(2,1)S(1)}, u32[]{:S(2)}, u32[]{:S(2)}) async-start(s16[4,64,1664]{2,1,0:T(8,128)(2,1)} %shard_map.104), calls=%async_computation.1 | async-start | bytes 1703936 | tf_op jit(solution)/shard_map/all_to_all | solution.py:321
  56.7 0.1 add.49
  56.8 0.1 and.41
  56.9 0.1 sub.44
  57.0 9.6 %all-to-all-done.1.parts_ref = s16[4,64,1664]{2,1,0:T(8,128)(2,1)S(1)} async-done(((s16[4,64,1664]{2,1,0:T(8,128)(2,1)}), s16[4,64,1664]{2,1,0:T(8,128)(2,1)S(1)}, u32[]{:S(2)}, u32[]{:S(2)}) %all-to-all-start.1) | async-done | bytes 852000 | tf_op jit(solution)/shard_map/all_to_all | solution.py:321
  66.6 0.8 shard_map.105
  67.4 1.9 %collective-permute-start.1 = (bf16[16,128]{1,0:T(8,128)(2,1)S(1)}, bf16[16,128]{1,0:T(8,128)(2,1)S(1)}, u32[]{:S(2)}, u32[]{:S(2)}) collective-permute-start(bf16[16,128]{1,0:T(8,128)(2,1)S(1)} %get-tuple-element.12.rows_ref), channel_id=1, source_target_pairs={{0,4},{4,0},{1,5},{5,1},{2,6},{6,2},{3,7},{7,3},{8,12},{12,8},{9,1... | collective-permute-start | bytes 12296 | tf_op jit(solution)/shard_map/ppermute | solution.py:341
  69.3 14.6 %all-gather = bf16[256,1664]{1,0:T(8,128)(2,1)S(1)} all-gather(bf16[64,1664]{1,0:T(8,128)(2,1)S(1)} %get-tuple-element.11), channel_id=2, replica_groups=mesh['section'=4,'z'=16,'core'=2,'x'=4] {'section'}, dimensions={0}, use_global_device_ids=true | all-gather | bytes 1064960 | tf_op jit(solution)/shard_map/all_gather | solution.py:342
  83.9 0.0 collective-permute-done.1.got_ref
  83.9 3.2 %shard_map.106 = bf16[4,64,2304]{2,1,0:T(8,128)(2,1)S(1)} custom-call(bf16[4,64,1664]{2,1,0:T(8,128)(2,1)S(1)} %bitcast.12, bf16[768,1024]{1,0:T(8,128)(2,1)S(1)} %copy-done, bf16[18432,1024]{1,0:T(8,128)(2,1)} %shard_map.103.far_ref, bf16[16,128]{1,0:T(8,128)(2,1)S(1)} %get-tuple-element.12.rows_ref, bf16[16,128]{1,0:T(8,128)(2,1)S(1)} %collective-permute-done.1.got_ref), custom_call_target="tpu_custom_call" | custom-call | tf_op jit(solution)/shard_map/pallas_call | solution.py:52
  87.1 18.3 %all_to_all.20.got_ref = bf16[4,64,2304]{2,1,0:T(8,128)(2,1)S(1)} all-to-all(bf16[4,64,2304]{2,1,0:T(8,128)(2,1)S(1)} %shard_map.106), channel_id=1, replica_groups=mesh['section'=4,'z'=16,'core'=2,'x'=4] {'x'}, dimensions={0} | all-to-all | bytes 2359296 | tf_op jit(solution)/shard_map/all_to_all | solution.py:354
  105.4 0.0 copy-start.6
  105.4 0.0 copy-start.4
  105.4 0.0 copy-start.5
  105.4 0.0 copy-start.1
  105.4 1.1 shard_map.107
  106.5 5.0 %all-to-all-start.3 = ((bf16[16,4,2304]{2,1,0:T(4,128)(2,1)}), bf16[16,4,2304]{2,1,0:T(4,128)(2,1)S(1)}, u32[]{:S(2)}, u32[]{:S(2)}) async-start(bf16[16,4,2304]{2,1,0:T(4,128)(2,1)} %shard_map.107), calls=%async_computation.3 | async-start | bytes 589824 | tf_op jit(solution)/shard_map/all_to_all | solution.py:356
  111.6 0.0 copy-done.6
  111.6 0.1 copy.19
  111.7 0.0 copy-done.4
  111.7 0.1 copy.20
  111.8 0.0 copy-done.5
  111.8 0.1 copy.21
  111.9 0.1 pad_maximum_fusion.token_ref
  112.0 0.7 convert_reduce_fusion
  112.7 16.5 %all-to-all-done.3.got_ref = bf16[16,4,2304]{2,1,0:T(4,128)(2,1)S(1)} async-done(((bf16[16,4,2304]{2,1,0:T(4,128)(2,1)}), bf16[16,4,2304]{2,1,0:T(4,128)(2,1)S(1)}, u32[]{:S(2)}, u32[]{:S(2)}) %all-to-all-start.3) | async-done | bytes 294944 | tf_op jit(solution)/shard_map/all_to_all | solution.py:356
  129.2 0.0 copy-done.1
  129.2 0.9 shard_map.108
  (10 shorter events, 0.1 us)
Async XLA Ops:
  0.6 19.3 %collective-permute-start = (bf16[768,1024]{1,0:T(8,128)(2,1)}, bf16[768,1024]{1,0:T(8,128)(2,1)S(1)}, u32[]{:S(2)}, u32[]{:S(2)}) collective-permute-start(bf16[768,1024]{1,0:T(8,128)(2,1)} %near_ref.3), channel_id=1, source_target_pairs={{0,4},{4,0},{1,5},{5,1},{2,6},{6,2},{3,7},{7,3},{8,12},{12,8},{9,1... | collective-permute-start | bytes 4718600 | tf_op jit(solution)/shard_map/ppermute | solution.py:299
  3.9 29.7 %all-to-all-start = ((bf16[16,4,1024]{2,1,0:T(4,128)(2,1)}), bf16[16,4,1024]{2,1,0:T(4,128)(2,1)S(1)}, u32[]{:S(2)}, u32[]{:S(2)}) async-start(bf16[16,4,1024]{2,1,0:T(4,128)(2,1)} %broadcast_in_dim.16), calls=%async_computation | async-start | bytes 262144 | tf_op jit(solution)/shard_map/all_to_all | solution.py:286
  19.9 27.1 %copy-start.2 = (f32[1024]{0:T(1024)S(1)}, f32[1024]{0:T(1024)}, u32[]{:S(2)}) copy-start(f32[1024]{0:T(1024)} %param.9) | copy-start | bytes 12292
  20.0 27.1 %copy-start.3 = (f32[1024]{0:T(1024)S(1)}, f32[1024]{0:T(1024)}, u32[]{:S(2)}) copy-start(f32[1024]{0:T(1024)} %param.10) | copy-start | bytes 12292
  20.0 27.1 %copy-start = (bf16[768,1024]{1,0:T(8,128)(2,1)S(1)}, bf16[768,1024]{1,0:T(8,128)(2,1)}, u32[]{:S(2)}) copy-start(bf16[768,1024]{1,0:T(8,128)(2,1)} %near_ref.3) | copy-start | bytes 4718596
  52.2 14.4 %all-to-all-start.1 = ((s16[4,64,1664]{2,1,0:T(8,128)(2,1)}), s16[4,64,1664]{2,1,0:T(8,128)(2,1)S(1)}, u32[]{:S(2)}, u32[]{:S(2)}) async-start(s16[4,64,1664]{2,1,0:T(8,128)(2,1)} %shard_map.104), calls=%async_computation.1 | async-start | bytes 1703936 | tf_op jit(solution)/shard_map/all_to_all | solution.py:321
  67.4 16.5 %collective-permute-start.1 = (bf16[16,128]{1,0:T(8,128)(2,1)S(1)}, bf16[16,128]{1,0:T(8,128)(2,1)S(1)}, u32[]{:S(2)}, u32[]{:S(2)}) collective-permute-start(bf16[16,128]{1,0:T(8,128)(2,1)S(1)} %get-tuple-element.12.rows_ref), channel_id=1, source_target_pairs={{0,4},{4,0},{1,5},{5,1},{2,6},{6,2},{3,7},{7,3},{8,12},{12,8},{9,1... | collective-permute-start | bytes 12296 | tf_op jit(solution)/shard_map/ppermute | solution.py:341
  105.4 6.2 %copy-start.6 = (s32[4]{0:T(128)S(1)}, s32[4]{0:T(128)}, u32[]{:S(2)}) copy-start(s32[4]{0:T(128)} %param.13) | copy-start | bytes 52
  105.4 6.3 %copy-start.4 = (f32[4]{0:T(128)S(1)}, f32[4]{0:T(128)}, u32[]{:S(2)}) copy-start(f32[4]{0:T(128)} %param.14) | copy-start | bytes 52
  105.4 6.4 %copy-start.5 = (f32[4]{0:T(128)S(1)}, f32[4]{0:T(128)}, u32[]{:S(2)}) copy-start(f32[4]{0:T(128)} %param.15) | copy-start | bytes 52
  105.4 23.7 %copy-start.1 = (bf16[4,1024]{1,0:T(4,128)(2,1)S(1)}, bf16[4,1024]{1,0:T(4,128)(2,1)}, u32[]{:S(2)}) copy-start(bf16[4,1024]{1,0:T(4,128)(2,1)} %hidden_ref.1) | copy-start | bytes 24580
  106.5 22.6 %all-to-all-start.3 = ((bf16[16,4,2304]{2,1,0:T(4,128)(2,1)}), bf16[16,4,2304]{2,1,0:T(4,128)(2,1)S(1)}, u32[]{:S(2)}, u32[]{:S(2)}) async-start(bf16[16,4,2304]{2,1,0:T(4,128)(2,1)} %shard_map.107), calls=%async_computation.3 | async-start | bytes 589824 | tf_op jit(solution)/shard_map/all_to_all | solution.py:356

commit v6 on v5

--- a/solution.py
+++ b/solution.py
@@ -11,7 +11,8 @@
 WIDTH = 1024
 VOCAB = 768
 PAIR = 2 * VOCAB
-PIECES = 4
+PIECES = 3
+PIECE = VOCAB // PIECES
 PARKED = 18432
 FULL = 4096
 CODED = PAIR + 128
@@ -84,7 +85,7 @@
 def pieces_of(source, target, arrived):
     copies = []
     for index in range(PIECES):
-        rows = pl.ds(index * (VOCAB // PIECES), VOCAB // PIECES)
+        rows = pl.ds(index * PIECE, PIECE)
         copies.append(
             pltpu.make_async_copy(source.at[rows], target.at[rows], arrived.at[index])
         )
@@ -93,8 +94,22 @@
     return copies
 
 
-def park(far_ref, out_ref, arrived):
-    for copy in pieces_of(far_ref, out_ref, arrived):
+def heads_of(near_ref, far_held, copies):
+    yield near_ref[...]
+    for index, copy in enumerate(copies):
+        copy.wait()
+        yield far_held[index * PIECE : (index + 1) * PIECE]
+
+
+def park(upper_ref, lower_ref, out_ref, arrived):
+    half = VOCAB // 2
+    copies = [
+        pltpu.make_async_copy(upper_ref, out_ref.at[0:half], arrived.at[0]),
+        pltpu.make_async_copy(lower_ref, out_ref.at[half:VOCAB], arrived.at[1]),
+    ]
+    for copy in copies:
+        copy.start()
+    for copy in copies:
         copy.wait()
 
 
@@ -118,9 +133,11 @@
     scale = 1.0 / unit_of(exponent)
     pieces = [jnp.round(part * scale) for part in logits]
     pieces.append(lanes(256, [exponent] + digits(squares) + digits(raw_values)))
-    for index, piece in enumerate(pieces):
+    start = 0
+    for piece in pieces:
         piece = piece.astype(jnp.int32).astype(jnp.int16)
-        columns = slice(index * VOCAB, min((index + 1) * VOCAB, CODED))
+        columns = slice(start, start + piece.shape[1])
+        start += piece.shape[1]
         for x in range(4):
             for s in range(4):
                 source = slice(x * 64 + s * 16, x * 64 + s * 16 + 16)
@@ -166,12 +183,10 @@
     ]
     chosen = jnp.concatenate(pieces, axis=0)
     product = wanted = 0.0
-    for index, ref in enumerate((near_ref, far_held)):
-        if ref is far_held:
-            for copy in copies:
-                copy.wait()
-        exps = chosen[:, index * VOCAB : (index + 1) * VOCAB].astype(f32)
-        head = ref[...]
+    start = 0
+    for head in heads_of(near_ref, far_held, copies):
+        exps = chosen[:, start : start + head.shape[0]].astype(f32)
+        start += head.shape[0]
         product += jnp.dot(
             jnp.maximum(exps, 0.0).astype(bf16), head, preferred_element_type=f32
         )
@@ -280,12 +295,6 @@
     logprobs_ref[...] = picked_row - (top_row + jnp.log(total_row))
 
 
-def spread(array, axis):
-    size = lax.axis_size(axis)
-    copies = jnp.broadcast_to(array[None], (size,) + array.shape)
-    return lax.all_to_all(copies, axis, 0, 0)
-
-
 def shards(
     hidden, norm_gain, value_weight, head_weight, targets, response_mask, loss_weight, value_target
 ):
@@ -296,17 +305,28 @@
     gain, value_row = norm_gain[None, :], value_weight[None, :]
     swap = [(0, 1), (1, 0)]
 
-    far_weight = lax.ppermute(head_weight, "core", swap)
+    copies, head_late = lax.optimization_barrier(
+        (jnp.broadcast_to(hidden[None], (16,) + hidden.shape), head_weight)
+    )
+    half = VOCAB // 2
+    upper = lax.ppermute(head_late[:half], "core", swap)
+    lower = lax.ppermute(head_late[half:], "core", swap)
     far_weight = pl.pallas_call(
         park,
         out_shape=jax.ShapeDtypeStruct((PARKED, WIDTH), bf16),
-        in_specs=[pl.BlockSpec(memory_space=pltpu.VMEM)],
+        in_specs=[pl.BlockSpec(memory_space=pltpu.VMEM)] * 2,
         out_specs=pl.BlockSpec(memory_space=pl.ANY),
-        scratch_shapes=[pltpu.SemaphoreType.DMA((PIECES,))],
+        scratch_shapes=[pltpu.SemaphoreType.DMA((2,))],
         compiler_params=pltpu.CompilerParams(vmem_limit_bytes=SCOPED),
-    )(far_weight)
-    by_z = spread(hidden, "z")
-    by_z, far_weight = lax.optimization_barrier((by_z, far_weight))
+    )(upper, lower)
+    by_z = lax.all_to_all(copies, "z", 0, 0)
+    block = targets.reshape(4, 2, 4, 4).transpose(1, 2, 0, 3).reshape(2, 64)
+    block = jnp.where(core == 0, block[0], block[1])
+    in_near, in_far = block - near * VOCAB, block - far * VOCAB
+    place = jnp.where((in_near >= 0) & (in_near < VOCAB), in_near, -1)
+    place = jnp.where((in_far >= 0) & (in_far < VOCAB), in_far + VOCAB, place)
+    place = place.reshape(64, 1)
+    by_z, far_weight, place = lax.optimization_barrier((by_z, far_weight, place))
     own = lax.all_gather(by_z.reshape(64, WIDTH), "x", axis=0, tiled=True)
     (sent,) = call(
         project,
@@ -320,11 +340,6 @@
     )
     parts = lax.all_to_all(sent, "section", 0, 0)
 
-    block = targets.reshape(4, 2, 4, 4).transpose(1, 2, 0, 3).reshape(2, 64)
-    block = jnp.where(core == 0, block[0], block[1])
-    in_near, in_far = block - near * VOCAB, block - far * VOCAB
-    place = jnp.where((in_near >= 0) & (in_near < VOCAB), in_near, -1)
-    place = jnp.where((in_far >= 0) & (in_far < VOCAB), in_far + VOCAB, place)
     exps, rows = pl.pallas_call(
         soften,
         out_shape=[
@@ -337,7 +352,7 @@
             pl.BlockSpec(memory_space=pltpu.VMEM),
         ],
         compiler_params=pltpu.CompilerParams(vmem_limit_bytes=SCOPED),
-    )(core.astype(jnp.int32).reshape(1), parts, place.reshape(64, 1))
+    )(core.astype(jnp.int32).reshape(1), parts, place)
     got_rows = lax.ppermute(rows, "core", swap)
     every = lax.all_gather(exps, "section", axis=0)
     (sent,) = call(

time: 131 us -> 133 us (1.015)
  blocking collectives: 46.3 us -> 60.3 us
  waiting for transfers between devices: 38.6 us -> 28.7 us
  starting transfers between devices: 28.6 us -> 26.9 us
    all_to_all x0 -> x1, blocking collectives: none -> 14.1 us  [shards(): parts = lax.all_to_all(sent, 'section', 0, 0)]
    all_to_all x2 -> x1, waiting for transfers between devices: 22.1 us -> 12.2 us  [shards(): by_z = lax.all_to_all(copies, 'z', 0, 0)]
    all_to_all x2 -> x1, starting transfers between devices: 19.7 us -> 15.2 us  [shards(): by_z = lax.all_to_all(copies, 'z', 0, 0)]
    ppermute x1 -> x2, starting transfers between devices: 1.92 us -> 4.33 us  [the longest x1 2.41 us: shards(): lower = lax.ppermute(head_late[half:], 'core', swap)]
    slice x0 -> x1, local copies, waits for them, and re-layouts: none -> 1.5 us  [shards(): lower = lax.ppermute(head_late[half:], 'core', swap)]
  transfers between devices with their start and end apart: 5 -> 5, of which waited for: 3 -> 2; matrix products, arithmetic and copies ran while one was open for 3% -> 1% of each run, Pallas kernels for 1% -> 1%
where the time goes in v6:
time: 133 us; the launch traced here: 132 us
  blocking collectives  60.3 us (45%)
  waiting for transfers between devices  28.7 us (22%)
  starting transfers between devices  26.9 us (20%)
  Pallas kernels  11.2 us (8%)
  local copies, waits for them, and re-layouts  3.61 us (3%)
    all_to_all x1, blocking collectives, shards(): got = lax.all_to_all(sent, 'x', 0, 0)  17.9 us
    all_to_all x1, waiting for transfers between devices, shards(): got = lax.all_to_all(sent, 'z', 0, 0)  16.5 us
    all_to_all x1, starting transfers between devices, shards(): by_z = lax.all_to_all(copies, 'z', 0, 0)  15.2 us
    all_gather x1, blocking collectives, shards(): every = lax.all_gather(exps, 'section', axis=0)  14.6 us
    all_to_all x1, blocking collectives, shards(): parts = lax.all_to_all(sent, 'section', 0, 0)  14.1 us
    all_gather x1, blocking collectives, shards(): own = lax.all_gather(by_z.reshape(64, WIDTH), 'x', axis=0, tiled=True)  13.7 us
    all_to_all x1, waiting for transfers between devices, shards(): by_z = lax.all_to_all(copies, 'z', 0, 0)  12.2 us
    pallas_call x4, Pallas kernels, call(): pl.pallas_call(body, out_shape=[jax.ShapeDtypeStruct(shape, dtype) for sh...  9.21 us
  transfers between devices with their start and end apart: 5, of which 2 were waited for; matrix products, arithmetic and copies ran while one was open for 1% of the time, Pallas kernels for 1%

profile of v6, /device:TPU:32, one launch (start us, length us, event | category | flops | bytes accessed | tf_op | source)
XLA Modules:
  0.0 132.3 jit_solution(5401304392443800459)
XLA Ops:
  0.6 1.4 %broadcast_in_dim.16 = bf16[16,4,1024]{2,1,0:T(4,128)(2,1)} broadcast(bf16[4,1024]{1,0:T(4,128)(2,1)} %hidden_ref.1), dimensions={1,2} | broadcast | bytes 139264 | tf_op jit(solution)/shard_map/broadcast_in_dim | solution.py:309
  2.0 0.0 copy-start.4
  2.0 1.5 %fusion = (bf16[384,1024]{1,0:T(8,128)(2,1)S(1)}, bf16[384,1024]{1,0:T(8,128)(2,1)S(1)}) fusion(bf16[768,1024]{1,0:T(8,128)(2,1)} %near_ref.3), kind=kLoop, calls=%fused_computation.9 | loop fusion | bytes 3145728 | tf_op jit(solution)/shard_map/slice | solution.py:313
  3.5 1.9 %collective-permute-start = (bf16[384,1024]{1,0:T(8,128)(2,1)S(1)}, bf16[384,1024]{1,0:T(8,128)(2,1)S(1)}, u32[]{:S(2)}, u32[]{:S(2)}) collective-permute-start(bf16[384,1024]{1,0:T(8,128)(2,1)S(1)} %get-tuple-element.24), channel_id=1, source_target_pairs={{0,4},{4,0},{1,5},{5,1},{2,6},{6,2},{3,7},{7,3},{8,12},{12,8},{9,1... | collective-permute-start | bytes 2359304 | tf_op jit(solution)/shard_map/ppermute | solution.py:312
  5.5 2.4 %collective-permute-start.1 = (bf16[384,1024]{1,0:T(8,128)(2,1)S(1)}, bf16[384,1024]{1,0:T(8,128)(2,1)S(1)}, u32[]{:S(2)}, u32[]{:S(2)}) collective-permute-start(bf16[384,1024]{1,0:T(8,128)(2,1)S(1)} %get-tuple-element.23), channel_id=1, source_target_pairs={{0,4},{4,0},{1,5},{5,1},{2,6},{6,2},{3,7},{7,3},{8,12},{12,8},{9,1... | collective-permute-start | bytes 2359304 | tf_op jit(solution)/shard_map/ppermute | solution.py:313
  7.9 15.2 %all-to-all-start = ((bf16[16,4,1024]{2,1,0:T(4,128)(2,1)}), bf16[16,4,1024]{2,1,0:T(4,128)(2,1)S(1)}, u32[]{:S(2)}, u32[]{:S(2)}) async-start(bf16[16,4,1024]{2,1,0:T(4,128)(2,1)} %broadcast_in_dim.16), calls=%async_computation | async-start | bytes 262144 | tf_op jit(solution)/shard_map/all_to_all | solution.py:322
  23.1 0.0 copy-done.4
  23.1 0.1 reshape.89
  23.3 0.1 add.49
  23.4 0.1 and.41
  23.5 0.1 sub.44
  23.6 0.0 copy-start.2
  23.6 0.0 copy-start.3
  23.6 0.0 collective-permute-done.upper_ref
  23.6 0.0 collective-permute-done.1.lower_ref
  23.6 0.0 copy-start
  23.6 1.2 shard_map.103.far_ref
  24.8 12.2 %all-to-all-done = bf16[16,4,1024]{2,1,0:T(4,128)(2,1)S(1)} async-done(((bf16[16,4,1024]{2,1,0:T(4,128)(2,1)}), bf16[16,4,1024]{2,1,0:T(4,128)(2,1)S(1)}, u32[]{:S(2)}, u32[]{:S(2)}) %all-to-all-start) | async-done | bytes 131104 | tf_op jit(solution)/shard_map/all_to_all | solution.py:322
  37.1 13.7 %all_gather.9.own_ref = bf16[256,1024]{1,0:T(8,128)(2,1)S(1)} all-gather(bf16[64,1024]{1,0:T(8,128)(2,1)S(1)} %reshape.90), channel_id=1, replica_groups=mesh['section'=4,'z'=16,'core'=2,'x'=4] {'x'}, dimensions={0}, use_global_device_ids=true | all-gather | bytes 655360 | tf_op jit(solution)/shard_map/all_gather | solution.py:330
  50.8 0.0 copy-done.2
  50.8 0.0 copy-done.3
  50.8 0.0 copy-done
  50.8 4.2 %shard_map.104 = s16[4,64,1664]{2,1,0:T(8,128)(2,1)S(1)} custom-call(bf16[256,1024]{1,0:T(8,128)(2,1)S(1)} %all_gather.9.own_ref, f32[1,1024]{1,0:T(1,128)S(1)} %bitcast.14, f32[1,1024]{1,0:T(1,128)S(1)} %bitcast.16, bf16[768,1024]{1,0:T(8,128)(2,1)S(1)} %copy-done, bf16[18432,1024]{1,0:T(8,128)(2,1)} %shard_map.103.far_ref), custom_call_target="tpu_custom_call" | custom-call | tf_op jit(solution)/shard_map/pallas_call | solution.py:53
  55.0 14.1 %all_to_all.20.parts_ref = s16[4,64,1664]{2,1,0:T(8,128)(2,1)S(1)} all-to-all(s16[4,64,1664]{2,1,0:T(8,128)(2,1)S(1)} %shard_map.104), channel_id=1, replica_groups=mesh['section'=4,'z'=16,'core'=2,'x'=4] {'section'}, dimensions={0} | all-to-all | bytes 1703936 | tf_op jit(solution)/shard_map/all_to_all | solution.py:341
  69.1 0.8 shard_map.105
  69.9 1.9 %collective-permute-start.2 = (bf16[16,128]{1,0:T(8,128)(2,1)S(1)}, bf16[16,128]{1,0:T(8,128)(2,1)S(1)}, u32[]{:S(2)}, u32[]{:S(2)}) collective-permute-start(bf16[16,128]{1,0:T(8,128)(2,1)S(1)} %get-tuple-element.18.rows_ref), channel_id=1, source_target_pairs={{0,4},{4,0},{1,5},{5,1},{2,6},{6,2},{3,7},{7,3},{8,12},{12,8},{9,1... | collective-permute-start | bytes 12296 | tf_op jit(solution)/shard_map/ppermute | solution.py:356
  71.8 14.6 %all-gather = bf16[256,1664]{1,0:T(8,128)(2,1)S(1)} all-gather(bf16[64,1664]{1,0:T(8,128)(2,1)S(1)} %get-tuple-element.17), channel_id=2, replica_groups=mesh['section'=4,'z'=16,'core'=2,'x'=4] {'section'}, dimensions={0}, use_global_device_ids=true | all-gather | bytes 1064960 | tf_op jit(solution)/shard_map/all_gather | solution.py:357
  86.4 0.0 collective-permute-done.2.got_ref
  86.4 3.0 %shard_map.106 = bf16[4,64,2304]{2,1,0:T(8,128)(2,1)S(1)} custom-call(bf16[4,64,1664]{2,1,0:T(8,128)(2,1)S(1)} %bitcast.12, bf16[768,1024]{1,0:T(8,128)(2,1)S(1)} %copy-done, bf16[18432,1024]{1,0:T(8,128)(2,1)} %shard_map.103.far_ref, bf16[16,128]{1,0:T(8,128)(2,1)S(1)} %get-tuple-element.18.rows_ref, bf16[16,128]{1,0:T(8,128)(2,1)S(1)} %collective-permute-done.2.got_ref), custom_call_target="tpu_custom_call" | custom-call | tf_op jit(solution)/shard_map/pallas_call | solution.py:53
  89.3 17.9 %all_to_all.21.got_ref = bf16[4,64,2304]{2,1,0:T(8,128)(2,1)S(1)} all-to-all(bf16[4,64,2304]{2,1,0:T(8,128)(2,1)S(1)} %shard_map.106), channel_id=1, replica_groups=mesh['section'=4,'z'=16,'core'=2,'x'=4] {'x'}, dimensions={0} | all-to-all | bytes 2359296 | tf_op jit(solution)/shard_map/all_to_all | solution.py:369
  107.2 0.0 copy-start.7
  107.2 0.0 copy-start.5
  107.2 0.0 copy-start.6
  107.2 0.0 copy-start.1
  107.2 1.1 shard_map.107
  108.4 5.4 %all-to-all-start.3 = ((bf16[16,4,2304]{2,1,0:T(4,128)(2,1)}), bf16[16,4,2304]{2,1,0:T(4,128)(2,1)S(1)}, u32[]{:S(2)}, u32[]{:S(2)}) async-start(bf16[16,4,2304]{2,1,0:T(4,128)(2,1)} %shard_map.107), calls=%async_computation.3 | async-start | bytes 589824 | tf_op jit(solution)/shard_map/all_to_all | solution.py:371
  113.8 0.0 copy-done.7
  113.8 0.1 copy.19
  113.9 0.0 copy-done.5
  113.9 0.1 copy.20
  114.0 0.0 copy-done.6
  114.0 0.1 copy.21
  114.1 0.1 pad_maximum_fusion.token_ref
  114.1 0.7 convert_reduce_fusion
  114.8 16.5 %all-to-all-done.3.got_ref = bf16[16,4,2304]{2,1,0:T(4,128)(2,1)S(1)} async-done(((bf16[16,4,2304]{2,1,0:T(4,128)(2,1)}), bf16[16,4,2304]{2,1,0:T(4,128)(2,1)S(1)}, u32[]{:S(2)}, u32[]{:S(2)}) %all-to-all-start.3) | async-done | bytes 294944 | tf_op jit(solution)/shard_map/all_to_all | solution.py:371
  131.3 0.0 copy-done.1
  131.3 0.9 shard_map.108
  (10 shorter events, 0.1 us)
Async XLA Ops:
  2.0 21.1 %copy-start.4 = (s32[128]{0:T(128)S(1)}, s32[128]{0:T(128)}, u32[]{:S(2)}) copy-start(s32[128]{0:T(128)} %param.12) | copy-start | bytes 1540
  3.5 20.1 %collective-permute-start = (bf16[384,1024]{1,0:T(8,128)(2,1)S(1)}, bf16[384,1024]{1,0:T(8,128)(2,1)S(1)}, u32[]{:S(2)}, u32[]{:S(2)}) collective-permute-start(bf16[384,1024]{1,0:T(8,128)(2,1)S(1)} %get-tuple-element.24), channel_id=1, source_target_pairs={{0,4},{4,0},{1,5},{5,1},{2,6},{6,2},{3,7},{7,3},{8,12},{12,8},{9,1... | collective-permute-start | bytes 2359304 | tf_op jit(solution)/shard_map/ppermute | solution.py:312
  5.5 18.1 %collective-permute-start.1 = (bf16[384,1024]{1,0:T(8,128)(2,1)S(1)}, bf16[384,1024]{1,0:T(8,128)(2,1)S(1)}, u32[]{:S(2)}, u32[]{:S(2)}) collective-permute-start(bf16[384,1024]{1,0:T(8,128)(2,1)S(1)} %get-tuple-element.23), channel_id=1, source_target_pairs={{0,4},{4,0},{1,5},{5,1},{2,6},{6,2},{3,7},{7,3},{8,12},{12,8},{9,1... | collective-permute-start | bytes 2359304 | tf_op jit(solution)/shard_map/ppermute | solution.py:313
  7.9 29.2 %all-to-all-start = ((bf16[16,4,1024]{2,1,0:T(4,128)(2,1)}), bf16[16,4,1024]{2,1,0:T(4,128)(2,1)S(1)}, u32[]{:S(2)}, u32[]{:S(2)}) async-start(bf16[16,4,1024]{2,1,0:T(4,128)(2,1)} %broadcast_in_dim.16), calls=%async_computation | async-start | bytes 262144 | tf_op jit(solution)/shard_map/all_to_all | solution.py:322
  23.6 27.2 %copy-start.2 = (f32[1024]{0:T(1024)S(1)}, f32[1024]{0:T(1024)}, u32[]{:S(2)}) copy-start(f32[1024]{0:T(1024)} %param.9) | copy-start | bytes 12292
  23.6 27.2 %copy-start.3 = (f32[1024]{0:T(1024)S(1)}, f32[1024]{0:T(1024)}, u32[]{:S(2)}) copy-start(f32[1024]{0:T(1024)} %param.10) | copy-start | bytes 12292
  23.6 27.2 %copy-start = (bf16[768,1024]{1,0:T(8,128)(2,1)S(1)}, bf16[768,1024]{1,0:T(8,128)(2,1)}, u32[]{:S(2)}) copy-start(bf16[768,1024]{1,0:T(8,128)(2,1)} %near_ref.3) | copy-start | bytes 4718596
  69.9 16.5 %collective-permute-start.2 = (bf16[16,128]{1,0:T(8,128)(2,1)S(1)}, bf16[16,128]{1,0:T(8,128)(2,1)S(1)}, u32[]{:S(2)}, u32[]{:S(2)}) collective-permute-start(bf16[16,128]{1,0:T(8,128)(2,1)S(1)} %get-tuple-element.18.rows_ref), channel_id=1, source_target_pairs={{0,4},{4,0},{1,5},{5,1},{2,6},{6,2},{3,7},{7,3},{8,12},{12,8},{9,1... | collective-permute-start | bytes 12296 | tf_op jit(solution)/shard_map/ppermute | solution.py:356
  107.2 6.5 %copy-start.7 = (s32[4]{0:T(128)S(1)}, s32[4]{0:T(128)}, u32[]{:S(2)}) copy-start(s32[4]{0:T(128)} %param.13) | copy-start | bytes 52
  107.2 6.6 %copy-start.5 = (f32[4]{0:T(128)S(1)}, f32[4]{0:T(128)}, u32[]{:S(2)}) copy-start(f32[4]{0:T(128)} %param.14) | copy-start | bytes 52
  107.2 6.7 %copy-start.6 = (f32[4]{0:T(128)S(1)}, f32[4]{0:T(128)}, u32[]{:S(2)}) copy-start(f32[4]{0:T(128)} %param.15) | copy-start | bytes 52
  107.2 24.1 %copy-start.1 = (bf16[4,1024]{1,0:T(4,128)(2,1)S(1)}, bf16[4,1024]{1,0:T(4,128)(2,1)}, u32[]{:S(2)}) copy-start(bf16[4,1024]{1,0:T(4,128)(2,1)} %hidden_ref.1) | copy-start | bytes 24580
  108.4 23.0 %all-to-all-start.3 = ((bf16[16,4,2304]{2,1,0:T(4,128)(2,1)}), bf16[16,4,2304]{2,1,0:T(4,128)(2,1)S(1)}, u32[]{:S(2)}, u32[]{:S(2)}) async-start(bf16[16,4,2304]{2,1,0:T(4,128)(2,1)} %shard_map.107), calls=%async_computation.3 | async-start | bytes 589824 | tf_op jit(solution)/shard_map/all_to_all | solution.py:371
